TPU v7x, 32 devices: a whole 2x2x4 slice. The times are simulated.
32 devices in a mesh: section: 4 (over x, core), dp: 8 (over z, y).
Axes of the slice: x: 2, y: 2, z: 4, core: 2. Of those that a mesh axis runs over, the one named last changes fastest.
Arguments:
- source: bfloat16 [32, 64, 1024], P('dp'), may hold values from -6 to 6
- target: bfloat16 [32, 64, 1024], P('dp'), may hold values from -6 to 6
- directions: int32 [32], P('dp'), may hold values from 0 to 15
- source_lengths: int32 [32], P('dp'), may hold values from 16 to 64, as said below
- target_lengths: int32 [32], P('dp'), may hold values from 16 to 64, as said below
- attn_in: bfloat16 [4, 1024, 3072], P('section', 'dp'), may hold values from -0.1875 to 0.1875
- attn_out: bfloat16 [4, 1024, 1024], P('section', 'dp'), may hold values from -0.75 to 0.75
- ffn_in: bfloat16 [4, 1024, 4096], P('section', 'dp'), may hold values from -0.1875 to 0.1875
- ffn_out: bfloat16 [4, 4096, 1024], P('section', 'dp'), may hold values from -0.09375 to 0.09375
- cross_weight: bfloat16 [4, 1024, 4096], P('section', 'dp')
- norm_gain: bfloat16 [4, 2, 1024], P('section'), may hold values from 0.25 to 1.75
- norm_bias: bfloat16 [4, 2, 1024], P('section'), may hold values from -4 to 4
- cross_norm: bfloat16 [4, 2, 1024], P('section')
- dir_table: float32 [16, 1024], replicated, may hold values from -6 to 6
- cotangent: bfloat16 [32, 64, 1024], P('dp'), may hold values from -6 to 6
Outputs:
- section_out: bfloat16 [4, 32, 64, 1024], P('section', 'dp')
- section_in_grad: bfloat16 [4, 32, 64, 1024], P('section', 'dp')
- attn_in_grad: float32 [4, 1024, 3072], P('section', 'dp')
- attn_out_grad: float32 [4, 1024, 1024], P('section', 'dp')
- ffn_in_grad: float32 [4, 1024, 4096], P('section', 'dp')
- ffn_out_grad: float32 [4, 4096, 1024], P('section', 'dp')
- cross_weight_grad: float32 [4, 1024, 4096], P('section', 'dp')
- norm_gain_grad: float32 [4, 2, 1024], P('section', None, 'dp')
- norm_bias_grad: float32 [4, 2, 1024], P('section', None, 'dp')
- cross_norm_grad: float32 [4, 2, 1024], P('section', None, 'dp')
- dir_table_grad: float32 [16, 1024], P('section', 'dp')
Inputs may be any that keep to these rules, and one draw needn't show every extreme that they name: `source_lengths`: the shortest and the longest source sentence each occur in every draw. `target_lengths`: the shortest and the longest target sentence each occur in every draw.
All inputs are finite; a program needn't handle non-finite values.
Results may differ from a plain program's by a relative error of at most 0.023.
Values may be sent and summed in bfloat16 or wider, within the bound.
A program may use at most 320 MiB of HBM per device.

v0:
```python
import math

import jax
import jax.numpy as jnp
from jax import lax
from jax.sharding import PartitionSpec as P

HEADS = 16


encoder_alpha = 3.42
decoder_alpha = 4.16
masked_score = -1000000000.0
norm_epsilon = 1e-05
highest = lax.Precision.HIGHEST


def shortened(value):
    return jax.tree.map(lambda a: a.astype(jnp.bfloat16) if a.dtype == jnp.float32 else a, value)


def shifted(value, axis, steps):
    count = lax.axis_size(axis)
    first, last = (max(0, -steps), min(count, count - steps))
    return lax.ppermute(value, axis, [(source, source + steps) for source in range(first, last)])


def spread_2(block, axis, holder):
    block = jnp.where(lax.axis_index(axis) == holder, block, jnp.zeros_like(block))
    return lax.psum(block, axis)


def product(operand, matrix):
    return jnp.dot(operand, matrix, preferred_element_type=jnp.float32)


def contract_rows(operand, matrix):
    return lax.dot_general(
        operand, matrix, (((0,), (0,)), ((), ())), preferred_element_type=jnp.float32
    )


def contract_cols(operand, matrix):
    return lax.dot_general(
        operand, matrix, (((1,), (1,)), ((), ())), preferred_element_type=jnp.float32
    )


def layer_norm(residual, gain_vec, bias_vec):
    centre = residual - jnp.mean(residual, axis=-1, keepdims=True)
    spread = jnp.mean(centre * centre, axis=-1, keepdims=True)
    return centre * lax.rsqrt(spread + norm_epsilon) * gain_vec + bias_vec


def split_heads(tensor):
    return tensor.reshape(tensor.shape[0], HEADS, tensor.shape[1] // HEADS)


def score_scale(tensor):
    return 1.0 / math.sqrt(tensor.shape[1] // HEADS)


def attend(queries, key_rows, values, allowed):
    scores = jnp.einsum(
        "qhd,khd->hqk",
        split_heads(queries),
        split_heads(key_rows),
        preferred_element_type=jnp.float32,
    ) * score_scale(queries)
    attn_probs = jax.nn.softmax(jnp.where(allowed, scores, masked_score), axis=-1)
    probs_low = attn_probs.astype(jnp.bfloat16)
    mixed_heads = jnp.einsum(
        "hqk,khd->qhd", probs_low, split_heads(values), preferred_element_type=jnp.float32
    )
    return (mixed_heads.reshape(queries.shape).astype(jnp.bfloat16), attn_probs, probs_low)


def attend_back(queries, key_rows, values, attn_probs, probs_low, grad_mixed):
    grad_heads = split_heads(grad_mixed)
    grad_probs = jnp.einsum(
        "qhd,khd->hqk", grad_heads, split_heads(values), preferred_element_type=jnp.float32
    )
    grad_values = jnp.einsum(
        "hqk,qhd->khd", probs_low, grad_heads, preferred_element_type=jnp.float32
    )
    grad_scores = attn_probs * (
        grad_probs - jnp.sum(grad_probs * attn_probs, axis=-1, keepdims=True)
    )
    scores_low = grad_scores.astype(jnp.bfloat16)
    scale_value = score_scale(queries)
    grad_queries = (
        jnp.einsum(
            "hqk,khd->qhd", scores_low, split_heads(key_rows), preferred_element_type=jnp.float32
        )
        * scale_value
    )
    grad_keys = (
        jnp.einsum(
            "hqk,qhd->khd", scores_low, split_heads(queries), preferred_element_type=jnp.float32
        )
        * scale_value
    )
    return (
        grad_queries.reshape(queries.shape),
        grad_keys.reshape(key_rows.shape),
        grad_values.reshape(values.shape),
    )


def self_forward(entry, qkv_weight, out_weight, allowed):
    model_width = entry.shape[1]
    qkv_rows = product(entry, qkv_weight).astype(jnp.bfloat16)
    projected = (
        qkv_rows[:, :model_width],
        qkv_rows[:, model_width : 2 * model_width],
        qkv_rows[:, 2 * model_width :],
    )
    mixed_heads, attn_probs, probs_low = attend(projected[0], projected[1], projected[2], allowed)
    return (product(mixed_heads, out_weight), (projected, mixed_heads, attn_probs, probs_low))


def self_backward(entry, qkv_weight, out_weight, stored, grad_branch):
    projected, mixed_heads, attn_probs, probs_low = stored
    branch_low = grad_branch.astype(jnp.bfloat16)
    grad_out_weight = contract_rows(mixed_heads, branch_low)
    grad_mixed = contract_cols(branch_low, out_weight).astype(jnp.bfloat16)
    gradients = attend_back(
        projected[0], projected[1], projected[2], attn_probs, probs_low, grad_mixed
    )
    grad_qkv = jnp.concatenate(gradients, axis=1).astype(jnp.bfloat16)
    return (contract_cols(grad_qkv, qkv_weight), contract_rows(entry, grad_qkv), grad_out_weight)


def cross_forward(hidden_low, memory_rows, cross_all, allowed):
    model_width = hidden_low.shape[1]
    queries = product(hidden_low, cross_all[:, :model_width]).astype(jnp.bfloat16)
    key_rows = product(memory_rows, cross_all[:, model_width : 2 * model_width]).astype(
        jnp.bfloat16
    )
    values = product(memory_rows, cross_all[:, 2 * model_width : 3 * model_width]).astype(
        jnp.bfloat16
    )
    mixed_heads, attn_probs, probs_low = attend(queries, key_rows, values, allowed)
    return (
        product(mixed_heads, cross_all[:, 3 * model_width :]),
        ((queries, key_rows, values), mixed_heads, attn_probs, probs_low),
    )


def cross_backward(hidden_low, memory_rows, cross_all, stored, grad_branch):
    model_width = hidden_low.shape[1]
    projected, mixed_heads, attn_probs, probs_low = stored
    branch_low = grad_branch.astype(jnp.bfloat16)
    grad_wout = contract_rows(mixed_heads, branch_low)
    grad_mixed = contract_cols(branch_low, cross_all[:, 3 * model_width :]).astype(jnp.bfloat16)
    gradients = attend_back(
        projected[0], projected[1], projected[2], attn_probs, probs_low, grad_mixed
    )
    grad_queries = gradients[0].astype(jnp.bfloat16)
    grad_keys = gradients[1].astype(jnp.bfloat16)
    grad_values = gradients[2].astype(jnp.bfloat16)
    grad_hidden = contract_cols(grad_queries, cross_all[:, :model_width])
    grad_memory = contract_cols(
        grad_keys, cross_all[:, model_width : 2 * model_width]
    ) + contract_cols(grad_values, cross_all[:, 2 * model_width : 3 * model_width])
    grad_cross = jnp.concatenate(
        (
            contract_rows(hidden_low, grad_queries),
            contract_rows(memory_rows, grad_keys),
            contract_rows(memory_rows, grad_values),
            grad_wout,
        ),
        axis=1,
    )
    return (grad_hidden, grad_memory, grad_cross)


def ffn_forward(hidden_low, in_weight, back_weight):
    pre_act = product(hidden_low, in_weight)
    act_low = jax.nn.gelu(pre_act).astype(jnp.bfloat16)
    return (product(act_low, back_weight), (pre_act, act_low))


def ffn_backward(hidden_low, in_weight, back_weight, stored, grad_branch):
    pre_act, act_low = stored
    branch_low = grad_branch.astype(jnp.bfloat16)
    grad_back = contract_rows(act_low, branch_low)
    grad_act = contract_cols(branch_low, back_weight)
    grad_pre = jax.vjp(jax.nn.gelu, pre_act)[1](grad_act)[0].astype(jnp.bfloat16)
    return (contract_cols(grad_pre, in_weight), contract_rows(hidden_low, grad_pre), grad_back)


def encoder_forward(entry, weights, norm_params, allowed):
    gain_rows, bias_rows = (norm_params[0], norm_params[1])
    branch, _ = self_forward(entry, weights[0], weights[1], allowed)
    hidden = layer_norm(
        encoder_alpha * entry.astype(jnp.float32) + branch, gain_rows[0], bias_rows[0]
    )
    ffn_branch, _ = ffn_forward(hidden.astype(jnp.bfloat16), weights[2], weights[3])
    return layer_norm(encoder_alpha * hidden + ffn_branch, gain_rows[1], bias_rows[1]).astype(
        jnp.bfloat16
    )


def encoder_backward(entry, grad_result, weights, norm_params, allowed):
    gain_rows, bias_rows = (norm_params[0], norm_params[1])
    branch, self_stored = self_forward(entry, weights[0], weights[1], allowed)
    hidden, first_norm = jax.vjp(
        layer_norm, encoder_alpha * entry.astype(jnp.float32) + branch, gain_rows[0], bias_rows[0]
    )
    hidden_low = hidden.astype(jnp.bfloat16)
    ffn_branch, ffn_stored = ffn_forward(hidden_low, weights[2], weights[3])
    _, second_norm = jax.vjp(
        layer_norm, encoder_alpha * hidden + ffn_branch, gain_rows[1], bias_rows[1]
    )
    grad_second, gain_last, bias_last = second_norm(grad_result.astype(jnp.float32))
    grad_hidden_low, grad_in, grad_back = ffn_backward(
        hidden_low, weights[2], weights[3], ffn_stored, grad_second
    )
    grad_first, gain_first, bias_first = first_norm(encoder_alpha * grad_second + grad_hidden_low)
    grad_entry, grad_qkv, grad_out = self_backward(
        entry, weights[0], weights[1], self_stored, grad_first
    )
    return (
        encoder_alpha * grad_first + grad_entry,
        (grad_qkv, grad_out, grad_in, grad_back),
        jnp.stack((gain_first, gain_last)),
        jnp.stack((bias_first, bias_last)),
    )


def decoder_forward(entry, memory_rows, weights, norm_params, allowed_pair):
    gain_rows, bias_rows, cross_gain, cross_bias = norm_params
    branch, _ = self_forward(entry, weights[0], weights[1], allowed_pair[0])
    first_hidden = layer_norm(
        decoder_alpha * entry.astype(jnp.float32) + branch, gain_rows[0], bias_rows[0]
    )
    cross_branch, _ = cross_forward(
        first_hidden.astype(jnp.bfloat16), memory_rows, weights[4], allowed_pair[1]
    )
    second_hidden = layer_norm(decoder_alpha * first_hidden + cross_branch, cross_gain, cross_bias)
    ffn_branch, _ = ffn_forward(second_hidden.astype(jnp.bfloat16), weights[2], weights[3])
    return layer_norm(
        decoder_alpha * second_hidden + ffn_branch, gain_rows[1], bias_rows[1]
    ).astype(jnp.bfloat16)


def decoder_backward(entry, grad_result, memory_rows, weights, norm_params, allowed_pair):
    gain_rows, bias_rows, cross_gain, cross_bias = norm_params
    branch, self_stored = self_forward(entry, weights[0], weights[1], allowed_pair[0])
    first_hidden, first_norm = jax.vjp(
        layer_norm, decoder_alpha * entry.astype(jnp.float32) + branch, gain_rows[0], bias_rows[0]
    )
    first_low = first_hidden.astype(jnp.bfloat16)
    cross_branch, cross_stored = cross_forward(first_low, memory_rows, weights[4], allowed_pair[1])
    second_hidden, second_norm = jax.vjp(
        layer_norm, decoder_alpha * first_hidden + cross_branch, cross_gain, cross_bias
    )
    second_low = second_hidden.astype(jnp.bfloat16)
    ffn_branch, ffn_stored = ffn_forward(second_low, weights[2], weights[3])
    _, third_norm = jax.vjp(
        layer_norm, decoder_alpha * second_hidden + ffn_branch, gain_rows[1], bias_rows[1]
    )
    grad_third, gain_last, bias_last = third_norm(grad_result.astype(jnp.float32))
    grad_second_low, grad_in, grad_back = ffn_backward(
        second_low, weights[2], weights[3], ffn_stored, grad_third
    )
    grad_second, cross_gain_grad, cross_bias_grad = second_norm(
        decoder_alpha * grad_third + grad_second_low
    )
    grad_first_low, grad_memory, grad_cross = cross_backward(
        first_low, memory_rows, weights[4], cross_stored, grad_second
    )
    grad_first, gain_first, bias_first = first_norm(decoder_alpha * grad_second + grad_first_low)
    grad_entry, grad_qkv, grad_out = self_backward(
        entry, weights[0], weights[1], self_stored, grad_first
    )
    weight_grads = (grad_qkv, grad_out, grad_in, grad_back, grad_cross)
    return (
        decoder_alpha * grad_first + grad_entry,
        grad_memory,
        weight_grads,
        jnp.stack((gain_first, gain_last)),
        jnp.stack((bias_first, bias_last)),
        jnp.stack((cross_gain_grad, cross_bias_grad)),
    )


def pick_row(array, position):
    return lax.dynamic_index_in_dim(array, position, 0, keepdims=False)


def put_row(array, position, value, active):
    return lax.dynamic_update_index_in_dim(
        array, jnp.where(active, value, pick_row(array, position)), position, 0
    )


def body(
    source,
    target,
    directions,
    source_lengths,
    target_lengths,
    attn_in,
    attn_out,
    ffn_in,
    ffn_out,
    cross_weight,
    norm_gain,
    norm_bias,
    cross_norm,
    dir_table,
    cotangent,
):
    section_count = lax.axis_size("section")
    dp_count = lax.axis_size("dp")
    half_sections = section_count // 2
    section_pos = lax.axis_index("section")
    decoder_side = section_pos >= half_sections
    micro_count, length, model_width = source.shape
    gathered = (
        lax.all_gather(attn_in, "dp", axis=1, tiled=True),
        lax.all_gather(attn_out, "dp", axis=1, tiled=True),
        lax.all_gather(ffn_in, "dp", axis=1, tiled=True),
        lax.all_gather(ffn_out, "dp", axis=1, tiled=True),
        lax.all_gather(cross_weight, "dp", axis=1, tiled=True),
    )
    weights = tuple((piece[0] for piece in gathered))
    norm_params = (
        norm_gain[0].astype(jnp.float32),
        norm_bias[0].astype(jnp.float32),
        cross_norm[0, 0].astype(jnp.float32),
        cross_norm[0, 1].astype(jnp.float32),
    )
    positions = jnp.arange(length)
    causal = positions[None, :] <= positions[:, None]
    routing = (directions[:, None] == jnp.arange(dir_table.shape[0])[None, :]).astype(jnp.float32)
    direction_rows = jnp.dot(routing, dir_table, precision=highest)
    clock_count = section_count + micro_count - 1

    def masks_of(micro_index):
        source_allowed = (positions < pick_row(source_lengths, micro_index))[None, None, :]
        target_allowed = (causal & (positions[None, :] < pick_row(target_lengths, micro_index)))[
            None
        ]
        return (source_allowed, target_allowed)

    def forward_clock(carry, moment):
        incoming, memory, section_inputs, outputs = carry
        micro_index = moment - section_pos
        active = (micro_index >= 0) & (micro_index < micro_count)
        micro_index = jnp.clip(micro_index, 0, micro_count - 1)
        source_allowed, target_allowed = masks_of(micro_index)
        first_target = (
            pick_row(target, micro_index).astype(jnp.float32)
            + pick_row(direction_rows, micro_index)[None, :]
        ).astype(jnp.bfloat16)
        entry = jnp.where(
            section_pos == 0,
            pick_row(source, micro_index),
            jnp.where(section_pos == half_sections, first_target, incoming),
        )

        def skip_forward(entry_rows, memory_rows):
            return jnp.zeros_like(entry_rows)

        def forward_encoder_branch(entry_rows, memory_rows):
            return encoder_forward(entry_rows, weights, norm_params, source_allowed)

        def forward_decoder_branch(entry_rows, memory_rows):
            return decoder_forward(
                entry_rows, memory_rows, weights, norm_params, (target_allowed, source_allowed)
            )

        branch_index = jnp.where(active, jnp.where(decoder_side, 2, 1), 0)
        result = lax.switch(
            branch_index,
            [skip_forward, forward_encoder_branch, forward_decoder_branch],
            entry,
            pick_row(memory, micro_index),
        )
        section_inputs = put_row(section_inputs, micro_index, entry, active)
        outputs = put_row(outputs, micro_index, result, active)
        incoming = jax.tree.map(
            lambda part, own: part.astype(own.dtype),
            shifted(shortened(result), "section", 1),
            result,
        )
        mem_slot = moment - (half_sections - 1)
        arrived = jax.tree.map(
            lambda part, own: part.astype(own.dtype),
            jax.tree.map(
                lambda part: spread_2(part, "section", half_sections - 1), shortened(result)
            ),
            result,
        )
        memory = put_row(
            memory,
            jnp.clip(mem_slot, 0, micro_count - 1),
            arrived,
            (mem_slot >= 0) & (mem_slot < micro_count),
        )
        return ((incoming, memory, section_inputs, outputs), None)

    rows_zero = jnp.zeros((micro_count, length, model_width), jnp.bfloat16)
    start = (jnp.zeros((length, model_width), jnp.bfloat16), rows_zero, rows_zero, rows_zero)
    (_, memory, section_inputs, outputs), _ = lax.scan(
        forward_clock, start, jnp.arange(clock_count)
    )
    gathered = (
        lax.all_gather(attn_in, "dp", axis=1, tiled=True),
        lax.all_gather(attn_out, "dp", axis=1, tiled=True),
        lax.all_gather(ffn_in, "dp", axis=1, tiled=True),
        lax.all_gather(ffn_out, "dp", axis=1, tiled=True),
        lax.all_gather(cross_weight, "dp", axis=1, tiled=True),
    )
    weights = tuple((piece[0] for piece in gathered))

    def backward_clock(carry, moment):
        incoming, memory_grads, memory_parts, totals, direction_total, input_grads = carry
        micro_index = moment - (section_count - 1 - section_pos)
        active = (micro_index >= 0) & (micro_index < micro_count)
        micro_index = jnp.clip(micro_index, 0, micro_count - 1)
        source_allowed, target_allowed = masks_of(micro_index)
        grad_entry_in = jnp.where(
            section_pos == section_count - 1,
            pick_row(cotangent, micro_index),
            jnp.where(
                section_pos == half_sections - 1, pick_row(memory_grads, micro_index), incoming
            ),
        )

        def skip_backward(entry_rows, grad_rows, memory_rows, running):
            return (
                jnp.zeros(entry_rows.shape, jnp.float32),
                running,
                jnp.zeros(memory_rows.shape, jnp.float32),
            )

        def backward_encoder_branch(entry_rows, grad_rows, memory_rows, running):
            grad_entry, weight_grads, gain_grads, bias_grads = encoder_backward(
                entry_rows, grad_rows, weights, norm_params, source_allowed
            )
            updated = (
                running[0] + weight_grads[0],
                running[1] + weight_grads[1],
                running[2] + weight_grads[2],
                running[3] + weight_grads[3],
                running[4],
                running[5] + gain_grads,
                running[6] + bias_grads,
                running[7],
            )
            return (grad_entry, updated, jnp.zeros(memory_rows.shape, jnp.float32))

        def backward_decoder_branch(entry_rows, grad_rows, memory_rows, running):
            grad_entry, grad_memory, weight_grads, gain_grads, bias_grads, cross_grads = (
                decoder_backward(
                    entry_rows,
                    grad_rows,
                    memory_rows,
                    weights,
                    norm_params,
                    (target_allowed, source_allowed),
                )
            )
            updated = (
                running[0] + weight_grads[0],
                running[1] + weight_grads[1],
                running[2] + weight_grads[2],
                running[3] + weight_grads[3],
                running[4] + weight_grads[4],
                running[5] + gain_grads,
                running[6] + bias_grads,
                running[7] + cross_grads,
            )
            return (grad_entry, updated, grad_memory)

        branch_index = jnp.where(active, jnp.where(decoder_side, 2, 1), 0)
        grad_entry, totals, grad_memory = lax.switch(
            branch_index,
            [skip_backward, backward_encoder_branch, backward_decoder_branch],
            pick_row(section_inputs, micro_index),
            grad_entry_in,
            pick_row(memory, micro_index),
            totals,
        )
        entry_grad_low = grad_entry.astype(jnp.bfloat16)
        input_grads = put_row(input_grads, micro_index, entry_grad_low, active)
        memory_parts = put_row(
            memory_parts, micro_index, pick_row(memory_parts, micro_index) + grad_memory, active
        )
        direction_part = (
            pick_row(routing, micro_index)[:, None]
            * jnp.sum(entry_grad_low.astype(jnp.float32), axis=0)[None, :]
        )
        direction_total = direction_total + jnp.where(
            active & (section_pos == half_sections), direction_part, 0.0
        )
        incoming = shifted(entry_grad_low, "section", -1)
        mem_slot = moment - (half_sections - 1)
        slot_index = jnp.clip(mem_slot, 0, micro_count - 1)
        summed = lax.psum(pick_row(memory_parts, slot_index).astype(jnp.bfloat16), "section")
        memory_grads = put_row(
            memory_grads, slot_index, summed, (mem_slot >= 0) & (mem_slot < micro_count)
        )
        return ((incoming, memory_grads, memory_parts, totals, direction_total, input_grads), None)

    ff_width = weights[2].shape[1]
    start_totals = (
        jnp.zeros((model_width, 3 * model_width), jnp.float32),
        jnp.zeros((model_width, model_width), jnp.float32),
        jnp.zeros((model_width, ff_width), jnp.float32),
        jnp.zeros((ff_width, model_width), jnp.float32),
        jnp.zeros((model_width, 4 * model_width), jnp.float32),
        jnp.zeros((2, model_width), jnp.float32),
        jnp.zeros((2, model_width), jnp.float32),
        jnp.zeros((2, model_width), jnp.float32),
    )
    start = (
        jnp.zeros((length, model_width), jnp.bfloat16),
        rows_zero,
        jnp.zeros((micro_count, length, model_width), jnp.float32),
        start_totals,
        jnp.zeros(dir_table.shape, jnp.float32),
        rows_zero,
    )
    (_, _, _, totals, direction_total, input_grads), _ = lax.scan(
        backward_clock, start, jnp.arange(clock_count)
    )
    norm_columns = jnp.concatenate((totals[5], totals[6]), axis=0).T
    cross_columns = totals[7].T
    shares = (
        lax.psum_scatter(
            totals[0].astype(jnp.bfloat16), "dp", scatter_dimension=0, tiled=True
        ).astype(jnp.float32),
        lax.psum_scatter(
            totals[1].astype(jnp.bfloat16), "dp", scatter_dimension=0, tiled=True
        ).astype(jnp.float32),
        lax.psum_scatter(
            totals[2].astype(jnp.bfloat16), "dp", scatter_dimension=0, tiled=True
        ).astype(jnp.float32),
        lax.psum_scatter(
            totals[3].astype(jnp.bfloat16), "dp", scatter_dimension=0, tiled=True
        ).astype(jnp.float32),
        lax.psum_scatter(
            totals[4].astype(jnp.bfloat16), "dp", scatter_dimension=0, tiled=True
        ).astype(jnp.float32),
        lax.psum_scatter(
            norm_columns.astype(jnp.bfloat16), "dp", scatter_dimension=0, tiled=True
        ).astype(jnp.float32),
        lax.psum_scatter(
            cross_columns.astype(jnp.bfloat16), "dp", scatter_dimension=0, tiled=True
        ).astype(jnp.float32),
    )
    gain_grad = shares[5][:, :2].T[None]
    bias_grad = shares[5][:, 2:].T[None]
    cross_norm_grad = shares[6].T[None]
    dir_count = dir_table.shape[0]
    dir_rows = dir_count // section_count
    dir_cols = model_width // dp_count
    dir_blocks = (
        direction_total.reshape(section_count, dir_rows, dp_count, dir_cols)
        .transpose(0, 2, 1, 3)
        .reshape(section_count * dp_count, dir_rows * dir_cols)
    )
    dir_mine = lax.psum_scatter(dir_blocks, ("section", "dp"), scatter_dimension=0, tiled=True)
    dir_table_grad = dir_mine.reshape(dir_rows, dir_cols)
    return (
        outputs[None],
        input_grads[None],
        shares[0][None],
        shares[1][None],
        shares[2][None],
        shares[3][None],
        shares[4][None],
        gain_grad,
        bias_grad,
        cross_norm_grad,
        dir_table_grad,
    )


def solution(mesh):
    placed = (
        P("dp", None, None),
        P("dp", None, None),
        P("dp"),
        P("dp"),
        P("dp"),
        P("section", "dp", None),
        P("section", "dp", None),
        P("section", "dp", None),
        P("section", "dp", None),
        P("section", "dp", None),
        P("section", None, None),
        P("section", None, None),
        P("section", None, None),
        P(),
        P("dp", None, None),
    )
    return jax.shard_map(
        body,
        mesh=mesh,
        in_specs=placed,
        out_specs=(
            P("section", "dp", None, None),
            P("section", "dp", None, None),
            P("section", "dp", None),
            P("section", "dp", None),
            P("section", "dp", None),
            P("section", "dp", None),
            P("section", "dp", None),
            P("section", None, "dp"),
            P("section", None, "dp"),
            P("section", None, "dp"),
            P("section", "dp"),
        ),
        check_vma=False,
    )
```

profile of v0, /device:TPU:0, one launch (start us, length us, event | category | flops | bytes accessed | tf_op | source)
XLA Modules:
  0.0 3365.0 jit_solution(6642114484412658689)
XLA Ops:
  14.9 47.3 %all-gather.8.cloned.1.call-done = bf16[1,1024,1024]{2,1,0:T(8,128)(2,1)} async-done(((bf16[1,128,1024]{2,1,0:T(8,128)(2,1)}), bf16[1,1024,1024]{2,1,0:T(8,128)(2,1)}) %all-gather.8.cloned.1.call-update) | async-done | bytes 2097168 | tf_op jit(solution)/shard_map/all_gather | solution.py:324
  62.2 99.7 %all-gather.6.cloned.1.call-done = bf16[1,1024,3072]{2,1,0:T(8,128)(2,1)} async-done(((bf16[1,128,3072]{2,1,0:T(8,128)(2,1)}), bf16[1,1024,3072]{2,1,0:T(8,128)(2,1)}) %all-gather.6.cloned.1.call-update) | async-done | bytes 6291472 | tf_op jit(solution)/shard_map/all_gather | solution.py:323
  161.9 125.3 %all-gather.10.cloned.1.call-done = bf16[1,1024,4096]{2,1,0:T(8,128)(2,1)} async-done(((bf16[1,128,4096]{2,1,0:T(8,128)(2,1)}), bf16[1,1024,4096]{2,1,0:T(8,128)(2,1)}) %all-gather.10.cloned.1.call-update) | async-done | bytes 8388624 | tf_op jit(solution)/shard_map/all_gather | solution.py:325
  287.2 125.1 %all-gather.12.cloned.1.call-done = bf16[1,4096,1024]{2,1,0:T(8,128)(2,1)} async-done(((bf16[1,512,1024]{2,1,0:T(8,128)(2,1)}), bf16[1,4096,1024]{2,1,0:T(8,128)(2,1)}) %all-gather.12.cloned.1.call-update) | async-done | bytes 8388624 | tf_op jit(solution)/shard_map/all_gather | solution.py:326
  412.3 125.1 %all-gather.14.cloned.1.call-done = bf16[1,1024,4096]{2,1,0:T(8,128)(2,1)} async-done(((bf16[1,128,4096]{2,1,0:T(8,128)(2,1)}), bf16[1,1024,4096]{2,1,0:T(8,128)(2,1)}) %all-gather.14.cloned.1.call-update) | async-done | bytes 8388624 | tf_op jit(solution)/shard_map/all_gather | solution.py:327
  540.0 480.3 %while.58 = (s32[]{:T(128)}, bf16[64,1024]{1,0:T(8,128)(2,1)S(1)}, bf16[4,64,1024]{2,1,0:T(8,128)(2,1)}, bf16[4,64,1024]{2,1,0:T(8,128)(2,1)}, bf16[4,64,1024]{2...) while((s32[]{:T(128)}, bf16[64,1024]{1,0:T(8,128)(2,1)S(1)}, ...), condition=%wide.region_21.22_spmd.clone.clone, body=%wide.region_0.21_spmd.clone.clone.sunk | while | flops 2196777472 | bytes 56410104 | solution.py:408
  545.9 18.1 conditional.8
  554.4 9.2 fusion.300
  569.1 25.6 all-reduce.7.cloned.1.call-done
  601.3 18.1 conditional.8
  609.8 9.2 fusion.300
  624.6 28.4 all-reduce.7.cloned.1.call-done
  660.4 18.1 conditional.8
  668.9 9.2 fusion.300
  683.7 43.0 %all-reduce.7.cloned.1.call-done = bf16[64,1024]{1,0:T(8,128)(2,1)} async-done(((bf16[64,1024]{1,0:T(8,128)(2,1)}), bf16[64,1024]{1,0:T(8,128)(2,1)}) %all-reduce.7.cloned.1.call-update) | async-done | bytes 131088 | tf_op jit(solution)/shard_map/while/body/eval_jaxpr/psum | solution.py:30
  734.1 18.1 conditional.8
  742.6 9.2 fusion.300
  757.4 43.0 %all-reduce.7.cloned.1.call-done = bf16[64,1024]{1,0:T(8,128)(2,1)} async-done(((bf16[64,1024]{1,0:T(8,128)(2,1)}), bf16[64,1024]{1,0:T(8,128)(2,1)}) %all-reduce.7.cloned.1.call-update) | async-done | bytes 131088 | tf_op jit(solution)/shard_map/while/body/eval_jaxpr/psum | solution.py:30
  807.9 18.4 collective-permute-start
  830.1 44.0 %all-reduce.7.cloned.1.call-done = bf16[64,1024]{1,0:T(8,128)(2,1)} async-done(((bf16[64,1024]{1,0:T(8,128)(2,1)}), bf16[64,1024]{1,0:T(8,128)(2,1)}) %all-reduce.7.cloned.1.call-update) | async-done | bytes 131088 | tf_op jit(solution)/shard_map/while/body/eval_jaxpr/psum | solution.py:30
  886.8 61.1 %all-reduce.7.cloned.1.call-done = bf16[64,1024]{1,0:T(8,128)(2,1)} async-done(((bf16[64,1024]{1,0:T(8,128)(2,1)}), bf16[64,1024]{1,0:T(8,128)(2,1)}) %all-reduce.7.cloned.1.call-update) | async-done | bytes 131088 | tf_op jit(solution)/shard_map/while/body/eval_jaxpr/psum | solution.py:30
  959.6 59.9 %all-reduce.7.cloned.1.call-done = bf16[64,1024]{1,0:T(8,128)(2,1)} async-done(((bf16[64,1024]{1,0:T(8,128)(2,1)}), bf16[64,1024]{1,0:T(8,128)(2,1)}) %all-reduce.7.cloned.1.call-update) | async-done | bytes 131088 | tf_op jit(solution)/shard_map/while/body/eval_jaxpr/psum | solution.py:30
  1023.5 6.1 broadcast_in_dim.286
  1032.2 7.8 broadcast.537
  1040.0 7.9 broadcast_in_dim.288
  1047.9 7.8 broadcast.537.clone
  1056.6 1397.5 %while.59 = (s32[]{:T(128)}, bf16[64,1024]{1,0:T(8,128)(2,1)}, bf16[4,64,1024]{2,1,0:T(8,128)(2,1)}, f32[4,64,1024]{2,1,0:T(8,128)}, f32[1024,3072]{0,1:T(8,128)...) while((s32[]{:T(128)}, bf16[64,1024]{1,0:T(8,128)(2,1)}, ...), condition=%wide.region_67.68_spmd.clone.clone, body=%wide.region_22.67_spmd.clone.clone.sunk | while | flops 6613713920 | bytes 398689920 | solution.py:529
  1076.9 197.2 %all-reduce.9.cloned.1.call-done = bf16[64,1024]{1,0:T(8,128)(2,1)} async-done(((bf16[64,1024]{1,0:T(8,128)(2,1)}), bf16[64,1024]{1,0:T(8,128)(2,1)}) %all-reduce.9.cloned.1.call-update) | async-done | bytes 131088 | tf_op jit(solution)/shard_map/while/body/eval_jaxpr/psum | solution.py:504
  1294.6 199.5 %all-reduce.9.cloned.1.call-done = bf16[64,1024]{1,0:T(8,128)(2,1)} async-done(((bf16[64,1024]{1,0:T(8,128)(2,1)}), bf16[64,1024]{1,0:T(8,128)(2,1)}) %all-reduce.9.cloned.1.call-update) | async-done | bytes 131088 | tf_op jit(solution)/shard_map/while/body/eval_jaxpr/psum | solution.py:504
  1515.6 199.7 %all-reduce.9.cloned.1.call-done = bf16[64,1024]{1,0:T(8,128)(2,1)} async-done(((bf16[64,1024]{1,0:T(8,128)(2,1)}), bf16[64,1024]{1,0:T(8,128)(2,1)}) %all-reduce.9.cloned.1.call-update) | async-done | bytes 131088 | tf_op jit(solution)/shard_map/while/body/eval_jaxpr/psum | solution.py:504
  1723.4 99.8 %conditional.9 = (f32[1024,3072]{0,1:T(8,128)}, f32[1024,1024]{1,0:T(8,128)}, f32[1024,4096]{1,0:T(8,128)}, f32[4096,1024]{1,0:T(8,128)}, f32[1024,4096]{0,1:T(8...) conditional(s32[]{:T(128)} %clamp.19, ...), branch_computations={%region_23.23_spmd, %region_24.39_spmd, %region_40.64_spmd} | conditional | flops 6613059584 | bytes 393403584 | solution.py:481
  1764.1 11.2 bitcast_add_fusion
  1780.5 14.1 convolution_add_fusion.5
  1794.6 13.9 convolution_add_fusion.4
  1835.2 101.6 %all-reduce.9.cloned.1.call-done = bf16[64,1024]{1,0:T(8,128)(2,1)} async-done(((bf16[64,1024]{1,0:T(8,128)(2,1)}), bf16[64,1024]{1,0:T(8,128)(2,1)}) %all-reduce.9.cloned.1.call-update) | async-done | bytes 131088 | tf_op jit(solution)/shard_map/while/body/eval_jaxpr/psum | solution.py:504
  1945.2 100.1 %conditional.9 = (f32[1024,3072]{0,1:T(8,128)}, f32[1024,1024]{1,0:T(8,128)}, f32[1024,4096]{1,0:T(8,128)}, f32[4096,1024]{1,0:T(8,128)}, f32[1024,4096]{0,1:T(8...) conditional(s32[]{:T(128)} %clamp.19, ...), branch_computations={%region_23.23_spmd, %region_24.39_spmd, %region_40.64_spmd} | conditional | flops 6613059584 | bytes 393403584 | solution.py:481
  1986.2 11.2 bitcast_add_fusion
  1997.4 5.2 convolution_add_fusion.6
  2002.6 14.1 convolution_add_fusion.5
  2016.7 13.9 convolution_add_fusion.4
  2057.3 100.4 %all-reduce.9.cloned.1.call-done = bf16[64,1024]{1,0:T(8,128)(2,1)} async-done(((bf16[64,1024]{1,0:T(8,128)(2,1)}), bf16[64,1024]{1,0:T(8,128)(2,1)}) %all-reduce.9.cloned.1.call-update) | async-done | bytes 131088 | tf_op jit(solution)/shard_map/while/body/eval_jaxpr/psum | solution.py:504
  2165.9 99.7 %conditional.9 = (f32[1024,3072]{0,1:T(8,128)}, f32[1024,1024]{1,0:T(8,128)}, f32[1024,4096]{1,0:T(8,128)}, f32[4096,1024]{1,0:T(8,128)}, f32[1024,4096]{0,1:T(8...) conditional(s32[]{:T(128)} %clamp.19, ...), branch_computations={%region_23.23_spmd, %region_24.39_spmd, %region_40.64_spmd} | conditional | flops 6613059584 | bytes 393403584 | solution.py:481
  2206.6 11.2 bitcast_add_fusion
  2223.1 14.1 convolution_add_fusion.5
  2237.2 13.9 convolution_add_fusion.4
  2277.7 26.7 all-reduce.9.cloned.1.call-done
  2311.9 100.1 %conditional.9 = (f32[1024,3072]{0,1:T(8,128)}, f32[1024,1024]{1,0:T(8,128)}, f32[1024,4096]{1,0:T(8,128)}, f32[4096,1024]{1,0:T(8,128)}, f32[1024,4096]{0,1:T(8...) conditional(s32[]{:T(128)} %clamp.19, ...), branch_computations={%region_23.23_spmd, %region_24.39_spmd, %region_40.64_spmd} | conditional | flops 6613059584 | bytes 393403584 | solution.py:481
  2352.9 11.2 bitcast_add_fusion
  2364.2 5.2 convolution_add_fusion.6
  2369.4 14.1 convolution_add_fusion.5
  2383.5 13.9 convolution_add_fusion.4
  2424.0 26.6 all-reduce.9.cloned.1.call-done
  2461.7 10.1 copy.211
  2471.8 9.1 convert_element_type.421
  2481.0 9.1 convert_element_type.420
  2490.2 13.9 copy.212
  2504.1 15.8 reduce-scatter.24.cloned.1.call-done
  2521.3 62.8 %reduce-scatter.22.cloned.1.call-done = bf16[128,4]{1,0:T(8,128)(2,1)} async-done(((bf16[1024,4]{1,0:T(8,128)(2,1)}), bf16[128,4]{1,0:T(8,128)(2,1)}) %reduce-scatter.22.cloned.1.call-update) | async-done | bytes 1040
  2585.5 121.3 %all-reduce.5.cloned.1.call-done = f32[32,512]{1,0:T(8,128)} async-done(((f32[32,512]{1,0:T(8,128)}), f32[32,512]{1,0:T(8,128)}) %all-reduce.5.cloned.1.call-update) | async-done | bytes 65552
  2708.1 71.3 %reduce-scatter.14.cloned.1.call-done = bf16[128,1024]{1,0:T(8,128)(2,1)} async-done(((bf16[1024,1024]{1,0:T(8,128)(2,1)}), bf16[128,1024]{1,0:T(8,128)(2,1)}) %reduce-scatter.14.cloned.1.call-update) | async-done | bytes 262160 | tf_op jit(solution)/shard_map/reduce_scatter | solution.py:538
  2781.2 118.7 %reduce-scatter.12.cloned.1.call-done = bf16[128,3072]{1,0:T(8,128)(2,1)} async-done(((bf16[1024,3072]{1,0:T(8,128)(2,1)}), bf16[128,3072]{1,0:T(8,128)(2,1)}) %reduce-scatter.12.cloned.1.call-update) | async-done | bytes 786448 | tf_op jit(solution)/shard_map/reduce_scatter | solution.py:535
  2902.3 149.4 %reduce-scatter.18.cloned.1.call-done = bf16[512,1024]{1,0:T(8,128)(2,1)} async-done(((bf16[4096,1024]{1,0:T(8,128)(2,1)}), bf16[512,1024]{1,0:T(8,128)(2,1)}) %reduce-scatter.18.cloned.1.call-update) | async-done | bytes 1048592 | tf_op jit(solution)/shard_map/reduce_scatter | solution.py:544
  3054.6 149.2 %reduce-scatter.16.cloned.1.call-done = bf16[128,4096]{1,0:T(8,128)(2,1)} async-done(((bf16[1024,4096]{1,0:T(8,128)(2,1)}), bf16[128,4096]{1,0:T(8,128)(2,1)}) %reduce-scatter.16.cloned.1.call-update) | async-done | bytes 1048592 | tf_op jit(solution)/shard_map/reduce_scatter | solution.py:541
  3206.5 148.7 %reduce-scatter.20.cloned.1.call-done = bf16[128,4096]{1,0:T(8,128)(2,1)} async-done(((bf16[1024,4096]{1,0:T(8,128)(2,1)}), bf16[128,4096]{1,0:T(8,128)(2,1)}) %reduce-scatter.20.cloned.1.call-update) | async-done | bytes 1048592 | tf_op jit(solution)/shard_map/reduce_scatter | solution.py:547
  (793 shorter events, 474.3 us)
Async XLA Ops:
  7.2 55.0 %all-gather.8.cloned.1.call-start = ((), (), s32[]{:S(2)}) async-start(), calls=%async_computation.8 | async-start | bytes 2359296 | tf_op jit(solution)/shard_map/all_gather | solution.py:324
  7.9 154.0 %all-gather.6.cloned.1.call-start = ((), (), s32[]{:S(2)}) async-start(), calls=%async_computation.7 | async-start | bytes 7077888 | tf_op jit(solution)/shard_map/all_gather | solution.py:323
  8.7 278.5 %all-gather.10.cloned.1.call-start = ((), (), s32[]{:S(2)}) async-start(), calls=%async_computation.9 | async-start | bytes 9437184 | tf_op jit(solution)/shard_map/all_gather | solution.py:325
  9.4 402.9 %all-gather.12.cloned.1.call-start = ((), (), s32[]{:S(2)}) async-start(), calls=%async_computation.10 | async-start | bytes 9437184 | tf_op jit(solution)/shard_map/all_gather | solution.py:326
  10.0 527.4 %all-gather.14.cloned.1.call-start = ((), (), s32[]{:S(2)}) async-start(), calls=%async_computation.11 | async-start | bytes 9437184 | tf_op jit(solution)/shard_map/all_gather | solution.py:327
  540.0 54.7 %all-reduce.7.cloned.1.call-start = ((), (), s32[]{:S(2)}) async-start(), calls=%async_computation.20 | async-start | bytes 262144 | tf_op jit(solution)/shard_map/while/body/eval_jaxpr/psum | solution.py:30
  563.9 31.5 collective-permute-start
  595.5 57.5 %all-reduce.7.cloned.1.call-start = ((), (), s32[]{:S(2)}) async-start(), calls=%async_computation.20 | async-start | bytes 262144 | tf_op jit(solution)/shard_map/while/body/eval_jaxpr/psum | solution.py:30
  619.4 35.2 %collective-permute-start = (bf16[64,1024]{1,0:T(8,128)(2,1)S(1)}, bf16[64,1024]{1,0:T(8,128)(2,1)S(1)}, u32[]{:S(2)}, u32[]{:S(2)}) collective-permute-start(bf16[64,1024]{1,0:T(8,128)(2,1)S(1)} %get-tuple-element.2515), channel_id=1, source_target_pairs={{0,8},{8,16},{16,24},{1,9},{9,17},{17,25},{2,10},{10,18},{18,26},{... | collective-permute-start | bytes 393224 | tf_op jit(solution)/shard_map/while/body/eval_jaxpr/ppermute | solution.py:25
  654.5 72.1 %all-reduce.7.cloned.1.call-start = ((), (), s32[]{:S(2)}) async-start(), calls=%async_computation.20 | async-start | bytes 262144 | tf_op jit(solution)/shard_map/while/body/eval_jaxpr/psum | solution.py:30
  678.5 49.8 %collective-permute-start = (bf16[64,1024]{1,0:T(8,128)(2,1)S(1)}, bf16[64,1024]{1,0:T(8,128)(2,1)S(1)}, u32[]{:S(2)}, u32[]{:S(2)}) collective-permute-start(bf16[64,1024]{1,0:T(8,128)(2,1)S(1)} %get-tuple-element.2515), channel_id=1, source_target_pairs={{0,8},{8,16},{16,24},{1,9},{9,17},{17,25},{2,10},{10,18},{18,26},{... | collective-permute-start | bytes 393224 | tf_op jit(solution)/shard_map/while/body/eval_jaxpr/ppermute | solution.py:25
  728.2 72.1 %all-reduce.7.cloned.1.call-start = ((), (), s32[]{:S(2)}) async-start(), calls=%async_computation.20 | async-start | bytes 262144 | tf_op jit(solution)/shard_map/while/body/eval_jaxpr/psum | solution.py:30
  752.2 49.8 %collective-permute-start = (bf16[64,1024]{1,0:T(8,128)(2,1)S(1)}, bf16[64,1024]{1,0:T(8,128)(2,1)S(1)}, u32[]{:S(2)}, u32[]{:S(2)}) collective-permute-start(bf16[64,1024]{1,0:T(8,128)(2,1)S(1)} %get-tuple-element.2515), channel_id=1, source_target_pairs={{0,8},{8,16},{16,24},{1,9},{9,17},{17,25},{2,10},{10,18},{18,26},{... | collective-permute-start | bytes 393224 | tf_op jit(solution)/shard_map/while/body/eval_jaxpr/ppermute | solution.py:25
  802.0 72.1 %all-reduce.7.cloned.1.call-start = ((), (), s32[]{:S(2)}) async-start(), calls=%async_computation.20 | async-start | bytes 262144 | tf_op jit(solution)/shard_map/while/body/eval_jaxpr/psum | solution.py:30
  807.9 67.8 %collective-permute-start = (bf16[64,1024]{1,0:T(8,128)(2,1)S(1)}, bf16[64,1024]{1,0:T(8,128)(2,1)S(1)}, u32[]{:S(2)}, u32[]{:S(2)}) collective-permute-start(bf16[64,1024]{1,0:T(8,128)(2,1)S(1)} %get-tuple-element.2515), channel_id=1, source_target_pairs={{0,8},{8,16},{16,24},{1,9},{9,17},{17,25},{2,10},{10,18},{18,26},{... | collective-permute-start | bytes 393224 | tf_op jit(solution)/shard_map/while/body/eval_jaxpr/ppermute | solution.py:25
  875.7 72.1 %all-reduce.7.cloned.1.call-start = ((), (), s32[]{:S(2)}) async-start(), calls=%async_computation.20 | async-start | bytes 262144 | tf_op jit(solution)/shard_map/while/body/eval_jaxpr/psum | solution.py:30
  881.6 66.9 %collective-permute-start = (bf16[64,1024]{1,0:T(8,128)(2,1)S(1)}, bf16[64,1024]{1,0:T(8,128)(2,1)S(1)}, u32[]{:S(2)}, u32[]{:S(2)}) collective-permute-start(bf16[64,1024]{1,0:T(8,128)(2,1)S(1)} %get-tuple-element.2515), channel_id=1, source_target_pairs={{0,8},{8,16},{16,24},{1,9},{9,17},{17,25},{2,10},{10,18},{18,26},{... | collective-permute-start | bytes 393224 | tf_op jit(solution)/shard_map/while/body/eval_jaxpr/ppermute | solution.py:25
  948.5 70.9 %all-reduce.7.cloned.1.call-start = ((), (), s32[]{:S(2)}) async-start(), calls=%async_computation.20 | async-start | bytes 262144 | tf_op jit(solution)/shard_map/while/body/eval_jaxpr/psum | solution.py:30
  954.4 65.7 %collective-permute-start = (bf16[64,1024]{1,0:T(8,128)(2,1)S(1)}, bf16[64,1024]{1,0:T(8,128)(2,1)S(1)}, u32[]{:S(2)}, u32[]{:S(2)}) collective-permute-start(bf16[64,1024]{1,0:T(8,128)(2,1)S(1)} %get-tuple-element.2515), channel_id=1, source_target_pairs={{0,8},{8,16},{16,24},{1,9},{9,17},{17,25},{2,10},{10,18},{18,26},{... | collective-permute-start | bytes 393224 | tf_op jit(solution)/shard_map/while/body/eval_jaxpr/ppermute | solution.py:25
  1056.6 217.5 %all-reduce.9.cloned.1.call-start = ((), (), s32[]{:S(2)}) async-start(), calls=%async_computation.21 | async-start | bytes 262144 | tf_op jit(solution)/shard_map/while/body/eval_jaxpr/psum | solution.py:504
  1065.8 209.0 %collective-permute-start.1 = (bf16[64,1024]{1,0:T(8,128)(2,1)}, bf16[64,1024]{1,0:T(8,128)(2,1)}, u32[]{:S(2)}, u32[]{:S(2)}) collective-permute-start(bf16[64,1024]{1,0:T(8,128)(2,1)} %get-tuple-element.2257), channel_id=1, source_target_pairs={{8,0},{16,8},{24,16},{9,1},{17,9},{25,17},{10,2},{18,10},{26,18},{... | collective-permute-start | bytes 393224 | tf_op jit(solution)/shard_map/while/body/eval_jaxpr/ppermute | solution.py:25
  1274.8 219.3 %all-reduce.9.cloned.1.call-start = ((), (), s32[]{:S(2)}) async-start(), calls=%async_computation.21 | async-start | bytes 262144 | tf_op jit(solution)/shard_map/while/body/eval_jaxpr/psum | solution.py:504
  1282.6 213.1 %collective-permute-start.1 = (bf16[64,1024]{1,0:T(8,128)(2,1)}, bf16[64,1024]{1,0:T(8,128)(2,1)}, u32[]{:S(2)}, u32[]{:S(2)}) collective-permute-start(bf16[64,1024]{1,0:T(8,128)(2,1)} %get-tuple-element.2257), channel_id=1, source_target_pairs={{8,0},{16,8},{24,16},{9,1},{17,9},{25,17},{10,2},{18,10},{26,18},{... | collective-permute-start | bytes 393224 | tf_op jit(solution)/shard_map/while/body/eval_jaxpr/ppermute | solution.py:25
  1495.7 219.6 %all-reduce.9.cloned.1.call-start = ((), (), s32[]{:S(2)}) async-start(), calls=%async_computation.21 | async-start | bytes 262144 | tf_op jit(solution)/shard_map/while/body/eval_jaxpr/psum | solution.py:504
  1503.6 213.3 %collective-permute-start.1 = (bf16[64,1024]{1,0:T(8,128)(2,1)}, bf16[64,1024]{1,0:T(8,128)(2,1)}, u32[]{:S(2)}, u32[]{:S(2)}) collective-permute-start(bf16[64,1024]{1,0:T(8,128)(2,1)} %get-tuple-element.2257), channel_id=1, source_target_pairs={{8,0},{16,8},{24,16},{9,1},{17,9},{25,17},{10,2},{18,10},{26,18},{... | collective-permute-start | bytes 393224 | tf_op jit(solution)/shard_map/while/body/eval_jaxpr/ppermute | solution.py:25
  1716.9 219.9 %all-reduce.9.cloned.1.call-start = ((), (), s32[]{:S(2)}) async-start(), calls=%async_computation.21 | async-start | bytes 262144 | tf_op jit(solution)/shard_map/while/body/eval_jaxpr/psum | solution.py:504
  1775.3 33.3 slice-start.4
  1780.5 14.1 copy-start.21
  1780.5 28.1 slice-start.5
  1794.6 14.0 copy-start.36
  1794.6 14.0 copy-start.37
  1794.6 14.0 copy-start.38
  1823.2 115.2 %collective-permute-start.1 = (bf16[64,1024]{1,0:T(8,128)(2,1)}, bf16[64,1024]{1,0:T(8,128)(2,1)}, u32[]{:S(2)}, u32[]{:S(2)}) collective-permute-start(bf16[64,1024]{1,0:T(8,128)(2,1)} %get-tuple-element.2257), channel_id=1, source_target_pairs={{8,0},{16,8},{24,16},{9,1},{17,9},{25,17},{10,2},{18,10},{26,18},{... | collective-permute-start | bytes 393224 | tf_op jit(solution)/shard_map/while/body/eval_jaxpr/ppermute | solution.py:25
  1938.6 219.0 %all-reduce.9.cloned.1.call-start = ((), (), s32[]{:S(2)}) async-start(), calls=%async_computation.21 | async-start | bytes 262144 | tf_op jit(solution)/shard_map/while/body/eval_jaxpr/psum | solution.py:504
  1997.4 33.3 slice-start.4
  2002.6 14.1 copy-start.21
  2002.6 28.1 slice-start.5
  2016.7 14.0 copy-start.37
  2016.7 14.0 copy-start.38
  2045.2 114.0 %collective-permute-start.1 = (bf16[64,1024]{1,0:T(8,128)(2,1)}, bf16[64,1024]{1,0:T(8,128)(2,1)}, u32[]{:S(2)}, u32[]{:S(2)}) collective-permute-start(bf16[64,1024]{1,0:T(8,128)(2,1)} %get-tuple-element.2257), channel_id=1, source_target_pairs={{8,0},{16,8},{24,16},{9,1},{17,9},{25,17},{10,2},{18,10},{26,18},{... | collective-permute-start | bytes 393224 | tf_op jit(solution)/shard_map/while/body/eval_jaxpr/ppermute | solution.py:25
  2159.4 145.0 %all-reduce.9.cloned.1.call-start = ((), (), s32[]{:S(2)}) async-start(), calls=%async_computation.21 | async-start | bytes 262144 | tf_op jit(solution)/shard_map/while/body/eval_jaxpr/psum | solution.py:504
  2217.9 33.3 slice-start.4
  2223.1 14.1 copy-start.21
  2223.1 28.1 slice-start.5
  2237.2 14.0 copy-start.37
  2237.2 14.0 copy-start.38
  2265.7 39.4 %collective-permute-start.1 = (bf16[64,1024]{1,0:T(8,128)(2,1)}, bf16[64,1024]{1,0:T(8,128)(2,1)}, u32[]{:S(2)}, u32[]{:S(2)}) collective-permute-start(bf16[64,1024]{1,0:T(8,128)(2,1)} %get-tuple-element.2257), channel_id=1, source_target_pairs={{8,0},{16,8},{24,16},{9,1},{17,9},{25,17},{10,2},{18,10},{26,18},{... | collective-permute-start | bytes 393224 | tf_op jit(solution)/shard_map/while/body/eval_jaxpr/ppermute | solution.py:25
  2305.4 145.2 %all-reduce.9.cloned.1.call-start = ((), (), s32[]{:S(2)}) async-start(), calls=%async_computation.21 | async-start | bytes 262144 | tf_op jit(solution)/shard_map/while/body/eval_jaxpr/psum | solution.py:504
  2364.1 33.3 slice-start.4
  2369.4 14.1 copy-start.21
  2369.4 28.1 slice-start.5
  2383.5 14.0 copy-start.36
  2383.5 14.0 copy-start.37
  2383.5 14.0 copy-start.38
  2412.0 39.3 %collective-permute-start.1 = (bf16[64,1024]{1,0:T(8,128)(2,1)}, bf16[64,1024]{1,0:T(8,128)(2,1)}, u32[]{:S(2)}, u32[]{:S(2)}) collective-permute-start(bf16[64,1024]{1,0:T(8,128)(2,1)} %get-tuple-element.2257), channel_id=1, source_target_pairs={{8,0},{16,8},{24,16},{9,1},{17,9},{25,17},{10,2},{18,10},{26,18},{... | collective-permute-start | bytes 393224 | tf_op jit(solution)/shard_map/while/body/eval_jaxpr/ppermute | solution.py:25
  2454.2 65.7 %reduce-scatter.24.cloned.1.call-start = ((), (), s32[]{:S(2)}) async-start(), calls=%async_computation.18 | async-start | bytes 294912
  2455.2 128.9 %reduce-scatter.22.cloned.1.call-start = ((), (), s32[]{:S(2)}) async-start(), calls=%async_computation.17 | async-start | bytes 294912
  2456.1 250.6 %all-reduce.5.cloned.1.call-start = ((), (), s32[]{:S(2)}) async-start(), calls=%async_computation.19 | async-start | bytes 131072
  2457.7 321.7 %reduce-scatter.14.cloned.1.call-start = ((), (), s32[]{:S(2)}) async-start(), calls=%async_computation.13 | async-start | bytes 2359296 | tf_op jit(solution)/shard_map/reduce_scatter | solution.py:538
  2461.6 438.3 %reduce-scatter.12.cloned.1.call-start = ((), (), s32[]{:S(2)}) async-start(), calls=%async_computation.12 | async-start | bytes 7077888 | tf_op jit(solution)/shard_map/reduce_scatter | solution.py:535
  2471.7 580.0 %reduce-scatter.18.cloned.1.call-start = ((), (), s32[]{:S(2)}) async-start(), calls=%async_computation.15 | async-start | bytes 9437184 | tf_op jit(solution)/shard_map/reduce_scatter | solution.py:544
  2480.9 722.8 %reduce-scatter.16.cloned.1.call-start = ((), (), s32[]{:S(2)}) async-start(), calls=%async_computation.14 | async-start | bytes 9437184 | tf_op jit(solution)/shard_map/reduce_scatter | solution.py:541
  2490.1 865.1 %reduce-scatter.20.cloned.1.call-start = ((), (), s32[]{:S(2)}) async-start(), calls=%async_computation.16 | async-start | bytes 9437184 | tf_op jit(solution)/shard_map/reduce_scatter | solution.py:547
  2504.0 853.9 %copy-start.1 = (f32[16,1024]{1,0:T(8,128)S(1)}, f32[16,1024]{1,0:T(8,128)}, u32[]{:S(2)}) copy-start(f32[16,1024]{1,0:T(8,128)} %param.38) | copy-start | bytes 196612
  (77 other events, 383.9 us)
Sparse Core Ops, SparseCore 0:
  10.2 51.9 all-gather.7
  64.4 97.5 all-gather.5
  164.0 123.1 all-gather.9
  289.2 123.1 all-gather.11
  414.3 123.1 all-gather.13
  566.1 28.6 all-reduce.6
  621.5 31.4 all-reduce.6
  680.6 46.0 all-reduce.6
  754.3 46.0 all-reduce.6
  827.1 46.9 all-reduce.6
  883.7 64.0 all-reduce.6
  956.5 62.8 all-reduce.6
  1072.2 201.8 all-reduce.8
  1289.0 205.0 all-reduce.8
  1510.0 205.2 all-reduce.8
  1829.6 107.1 all-reduce.8
  2051.6 105.9 all-reduce.8
  2272.1 32.2 all-reduce.8
  2418.4 32.1 all-reduce.8
  2458.6 61.2 reduce-scatter.23
  2523.8 60.2 reduce-scatter.21
  2590.2 116.5 all-reduce.4
  2710.9 68.4 reduce-scatter.13
  2782.8 117.0 reduce-scatter.11
  2903.5 148.1 reduce-scatter.17
  3055.7 147.9 reduce-scatter.15
  3207.2 147.9 reduce-scatter.19
where the time goes:
time: 3380 us; the launch traced here: 3370 us
  waiting for transfers between devices  2520 us (75%)
  matrix products  365 us (11%)
  local copies, waits for them, and re-layouts  204 us (6%)
  other arithmetic  155 us (5%)
  loops' own time  71 us (2%)
  starting transfers between devices  35.9 us (1%)
    psum x7, waiting for transfers between devices, backward_clock(): lax.psum(pick_row(memory_parts, slot_index).astype(jnp.bfloat16), 'section')  852 us
    psum x7, waiting for transfers between devices, spread_2(): return lax.psum(block, axis)  305 us
    unnamed x16, waiting for transfers between devices  203 us
    dot_general x16, matrix products, contract_rows(): lax.dot_general(operand, matrix, (((0,), (0,)), ((), ())), preferred_elem...  178 us
    reduce_scatter x1, waiting for transfers between devices, body(): lax.psum_scatter(totals[3].astype(jnp.bfloat16), 'dp', scatter_dimension=...  149 us
    reduce_scatter x1, waiting for transfers between devices, body(): lax.psum_scatter(totals[2].astype(jnp.bfloat16), 'dp', scatter_dimension=...  149 us
    reduce_scatter x1, waiting for transfers between devices, body(): lax.psum_scatter(totals[4].astype(jnp.bfloat16), 'dp', scatter_dimension=...  149 us
    all_gather x1, waiting for transfers between devices, body(): lax.all_gather(ffn_in, 'dp', axis=1, tiled=True)  125 us
  transfers between devices with their start and end apart: 41, of which 27 were waited for; matrix products, arithmetic and copies ran while one was open for 5% of the time, Pallas kernels for 0%

commit v1 on v0

v1 whole, which is shorter than its diff:
```python
import math
import types

import jax
import jax.numpy as jnp
from jax import lax
from jax.experimental import pallas as pl
from jax.experimental.pallas import tpu as pltpu
from jax.sharding import PartitionSpec as P

HEADS = 16
GROUP = 8
PAIR_BIT = 1
ENCODER_ALPHA = 3.42
DECODER_ALPHA = 4.16
MASKED = -1000000000.0
EPSILON = 1e-05
MESH = pl.DeviceIdType.MESH
f32, bf16 = jnp.float32, jnp.bfloat16
NN, NT, TN = (((1,), (0,)), ((), ())), (((1,), (1,)), ((), ())), (((0,), (0,)), ((), ()))
ATTN, CROSS, FFN = 0, 1, 2
QKV, FIN, FOUT, CQKV, OUT, COUT = range(6)
KIND_MATS = {ATTN: (QKV, OUT), CROSS: (CQKV, COUT), FFN: (FIN, FOUT)}
DECODER_MATS = (CQKV, COUT)


def dot(a, b, dims):
    return lax.dot_general(a, b, dims, preferred_element_type=f32)


def dv(a, b):
    return a // b if isinstance(a, int) else lax.div(a, jnp.int32(b))


def rm(a, b):
    return a % b if isinstance(a, int) else lax.rem(a, jnp.int32(b))


def mul(a, b):
    return pl.multiple_of(a * b, b)


def make_plan(sections, dp_count, pairs, seq, width, ff, directions):
    p = types.SimpleNamespace()
    p.NS, p.ND, p.L, p.half = sections, dp_count, sections, sections // 2
    p.pairs, p.seq, p.D, p.FF, p.R = pairs, seq, width, ff, pairs * seq
    p.tz = 2 if sections < GROUP and dp_count >= 4 else 1
    p.TPN = sections * p.tz
    p.K = p.TPN // 2
    p.RR = p.R // p.TPN
    p.CW = width // p.TPN
    p.HPR = HEADS // p.TPN
    p.FB = ff // p.TPN
    p.rb = width // dp_count
    p.fb = ff // dp_count // p.TPN
    p.q = dp_count // p.TPN
    p.NU = dp_count // p.tz
    p.C = p.NU // p.q
    p.cw = width // p.C
    p.NB = dp_count.bit_length() - 1
    if p.tz == 2:
        p.steps = [b for b in reversed(range(p.NB)) if b != PAIR_BIT]
    else:
        p.steps = list(range(p.NB))
    p.nst = len(p.steps)
    p.T = 2 * p.half + 3 * (p.L - p.half)
    p.NDIR = directions
    p.dir_rows = directions // sections
    p.cols = width // dp_count
    return p


def build(p):
    NS, ND, L, half, TPN, K, RR, R, D = p.NS, p.ND, p.L, p.half, p.TPN, p.K, p.RR, p.R, p.D
    CW, FB, NU, NB, nst, T, tz, q = p.CW, p.FB, p.NU, p.NB, p.nst, p.T, p.tz, p.q
    NH, LD = tz, p.L - p.half
    HB = K * RR
    C, cw = p.C, p.cw
    mat_block = {
        QKV: (p.rb, 3 * CW),
        FIN: (p.rb, FB),
        FOUT: (p.fb, D),
        CQKV: (p.rb, 3 * CW),
        OUT: (p.rb, cw),
        COUT: (p.rb, cw),
    }
    all_bits = list(reversed(range(NB)))
    mat_bits = {m: [b for b in all_bits if b in p.steps] if m in (OUT, COUT) else all_bits for m in mat_block}
    two = {m: (2,) * len(mat_bits[m]) for m in mat_block}
    back_steps = p.steps[::-1]

    vm, dma = pltpu.VMEM, pltpu.SemaphoreType.DMA
    scratch = dict(
        norms=vm((NS, 8, D), f32),
        aux=vm((NH, 8, R), f32),
        dirw=vm((NH, p.pairs, p.NDIR, 128), f32),
        cotb=vm((NH, RR, D), bf16),
        xbuf=vm((L + 2, NH, R, D), bf16),
        hb=vm((L, NH, R, D), bf16),
        h1b=vm((LD, NH, R, D), bf16),
        qkv=vm((L, NH, R, 3 * CW), bf16),
        cqkv=vm((LD, NH, R, 3 * CW), bf16),
        osv=vm((L, NH, R, CW), bf16),
        cosv=vm((LD, NH, R, CW), bf16),
        pre=vm((L, NH, R, FB), bf16),
        act=vm((R, FB), bf16),
        zs=vm((T, NH, RR, D), bf16),
        rstd=vm((T, NH, RR, 128), f32),
        res=vm((NH, RR, D), f32),
        gy=vm((NH, RR, D), f32),
        gag=vm((2, NH, R, D), bf16),
        gxo=vm((L, NH, RR, D), bf16),
        gmem=vm((NH, R, D), f32),
        gqkv=vm((NH, R, 3 * CW), bf16),
        gpre=vm((NH, R, FB), bf16),
        actb=vm((NH, R, FB), bf16),
        rsas=vm((2, NH, HB, D), bf16),
        rsar=vm((2, NH, HB, D), bf16),
        rsp=vm((NH, HB, D), f32),
        rsbs=vm((2, NH, K, RR, D), bf16),
        rsbr=vm((2, NH, K, RR, D), bf16),
        small=vm((NS, 16, D), f32),
        sm1=vm((TPN, NU * p.cols // 128, 16, 128), f32),
        sm1r=vm((TPN, NU * p.cols // 128, 16, 128), f32),
        sm2=vm((NU, 16, 128), f32),
        sm2r=vm((NU, 16, 128), f32),
        smo=vm((16, 128), f32),
        init_l=dma((5,)),
        init_s=dma((5,)),
        init_r=dma((5,)),
        norm_s=dma((NS,)),
        norm_r=dma((NS,)),
        a2a_s=dma((4, TPN)),
        a2a_r=dma((6, L, tz)),
        wo_s=dma((2, C)),
        ag_s=dma((nst, 6, L)),
        ag_r=dma((nst, 6, L)),
        tpa_s=dma((2, NH, K)),
        tpa_r=dma((2, NH, K)),
        tpf_s=dma((2, NH, K)),
        tpf_r=dma((2, NH, K)),
        rsa_s=dma((2, NH)),
        rsa_r=dma((2, NH)),
        rsb_s=dma((2, NH, K)),
        rsb_r=dma((2, NH, K)),
        gr_s=dma((nst, 6)),
        gr_r=dma((nst, 6)),
        credit=pltpu.SemaphoreType.REGULAR((nst, 3)),
        home_s=dma((6, tz)),
        home_r=dma((6, max(TPN, C))),
        sig_s=dma((L, NH)),
        sig_r=dma((TPN,)),
        sm1_s=dma((TPN,)),
        sm1_rs=dma((TPN,)),
        sm2_s=dma((NU,)),
        sm2_rs=dma((NU,)),
        out_l=dma((L,)),
        smo_l=dma((1,)),
    )
    for m, block in mat_block.items():
        scratch["w%d" % m] = vm((LD if m in DECODER_MATS else L,) + two[m] + block, bf16)
        scratch["g%d" % m] = vm(two[m] + block, bf16)
        scratch["st%d" % m] = vm((2 ** (len(two[m]) - nst),) + block, bf16)
        for j in range(1, nst + 1):
            scratch["r%d_%d" % (m, j)] = vm(two[m][j:] + block, bf16)
    in_names = ["src", "x2", "cot", "auxi", "dirwi", "normsi", "aq", "ai", "af", "ac", "woi", "wcoi"]
    out_names = ["out", "sig", "hq", "hi", "hf", "hc", "hwo", "hwco", "smout"]
    scratch_names = list(scratch)

    def kernel(*refs):
        n = types.SimpleNamespace(**dict(zip(in_names + out_names + scratch_names, refs)))
        W = {m: getattr(n, "w%d" % m) for m in mat_block}
        A = {QKV: n.aq, FIN: n.ai, FOUT: n.af, CQKV: n.ac}
        H = {QKV: n.hq, FIN: n.hi, FOUT: n.hf, CQKV: n.hc, OUT: n.hwo, COUT: n.hwco}
        G = {m: getattr(n, "g%d" % m) for m in mat_block}
        ST = {m: getattr(n, "st%d" % m) for m in mat_block}
        RB = {m: [None] + [getattr(n, "r%d_%d" % (m, j)) for j in range(1, nst + 1)] for m in mat_block}
        s, d = lax.axis_index("section"), lax.axis_index("dp")
        core, x = rm(s, 2), dv(s, 2)
        bit = [rm(dv(d, 1 << b), 2) for b in range(NB)]
        zl = bit[PAIR_BIT] if tz == 2 else 0
        k = zl * (NS // 2) + x
        r = core * K + k
        g = dv(d, 4) * 2 + rm(d, 2) if tz == 2 else d

        def place(rank, group):
            c2, k2 = dv(rank, K), rm(rank, K)
            x2, z2 = rm(k2, NS // 2), dv(k2, NS // 2)
            d2 = dv(group, 2) * 4 + z2 * 2 + rm(group, 2) if tz == 2 else group
            return (x2 * 2 + c2, d2)

        def with_bit(b, value):
            return d + (value - bit[b]) * (1 << b)

        def remote(src, dst, send, recv, device):
            return pltpu.make_async_remote_copy(
                src_ref=src, dst_ref=dst, send_sem=send, recv_sem=recv, device_id=device, device_id_type=MESH
            )

        def local(src, dst, sem):
            return pltpu.make_async_copy(src, dst, sem)

        def wait(ref, sem):
            pltpu.make_async_copy(ref, ref, sem).wait()

        sibling = place((1 - core) * K + k, g)

        barrier = pltpu.get_barrier_semaphore()
        total = NS * ND
        me = s * ND + d

        @pl.loop(1, total)
        def _(j):
            other = rm(me + j, total)
            pl.semaphore_signal(barrier, inc=1, device_id=(dv(other, ND), rm(other, ND)), device_id_type=MESH)

        pl.semaphore_wait(barrier, total - 1)

        own = pl.ds(mul(r, RR), RR)
        for j in range(1, NS):
            to = rm(s + j, NS)
            remote(n.normsi, n.norms.at[s], n.norm_s.at[j], n.norm_r.at[j], (to, d)).start()
        local(n.normsi, n.norms.at[s], n.norm_s.at[0]).start()
        other_rank = core * K + (1 - zl) * (NS // 2) + x
        other_rows = pl.ds(mul(other_rank, RR), RR)
        pair_dev = (s, with_bit(PAIR_BIT, 1 - zl)) if tz == 2 else None
        firsts = [
            (n.src, n.xbuf.at[0, zl], n.src, n.xbuf.at[0, zl]),
            (n.x2, n.xbuf.at[half + 1, zl], n.x2, n.xbuf.at[half + 1, zl]),
            (n.auxi, n.aux.at[zl], n.auxi, n.aux.at[zl]),
            (n.dirwi, n.dirw.at[zl], n.dirwi, n.dirw.at[zl]),
            (n.cot.at[own], n.cotb.at[zl], n.cot.at[other_rows], n.cotb.at[zl]),
        ]

        def first_start(i):
            a, b, c, e = firsts[i]
            local(a, b, n.init_l.at[i]).start()
            if tz == 2:
                remote(c, e, n.init_s.at[i], n.init_r.at[i], pair_dev).start()

        def first_wait(i):
            a, b, c, e = firsts[i]
            wait(b, n.init_l.at[i])
            if tz == 2:
                wait(e, n.init_s.at[i])
                wait(e, n.init_r.at[i])

        first_start(2)
        first_start(0)

        def wreg(m, l, fixed):
            idx = tuple(fixed.get(b, slice(None)) for b in mat_bits[m])
            return W[m].at[(l - half if m in DECODER_MATS else l,) + idx]

        mine = {b: bit[b] for b in range(NB)}

        def a2a_start(m):
            dst = wreg(m, s, mine)
            local(A[m].at[r], dst, n.a2a_r.at[m, s, zl]).start()
            for j in range(1, TPN):
                to = rm(r + j, TPN)
                remote(A[m].at[to], dst, n.a2a_s.at[m, j], n.a2a_r.at[m, s, zl], place(to, g)).start()

        def group_bits(m, group):
            count = len(mat_bits[m])
            return tuple(rm(dv(group, 1 << (count - 1 - i)), 2) for i in range(count))

        def out_pieces(m):
            rank = dv(d, q)
            for c in range(C):
                group = rm(d, q) * C + c
                yield c, pl.ds(c * cw, cw), group, rank, (rank == r) & (group == g)

        def out_start(m, src):
            for c, span, group, rank, here in out_pieces(m):
                dst = W[m].at[(s - half if m in DECODER_MATS else s,) + group_bits(m, group)]

                @pl.when(here)
                def _():
                    local(src.at[:, span], dst, n.a2a_r.at[m, s, 0]).start()

                @pl.when(jnp.logical_not(here))
                def _():
                    remote(src.at[:, span], dst, n.wo_s.at[m - OUT, c], n.a2a_r.at[m, s, 0], place(rank, group)).start()

        a2a_start(QKV)
        out_start(OUT, n.woi)
        a2a_start(FIN)
        a2a_start(FOUT)

        @pl.when(s >= half)
        def _():
            a2a_start(CQKV)
            out_start(COUT, n.wcoi)

        first_start(1)
        first_start(4)
        first_start(3)

        def kind_layer(t):
            td = jnp.maximum(t - 2 * half, 0)
            is_enc = t < 2 * half
            tt = jnp.maximum(t, 0)
            kind = jnp.where(is_enc, 2 * rm(tt, 2), rm(td, 3))
            layer = jnp.where(is_enc, dv(tt, 2), half + dv(td, 3))
            return kind, layer

        def groups(t, fn, after_kind=None):
            valid = (t >= 0) & (t < T)
            kind, layer = kind_layer(t)
            for kd, mats in KIND_MATS.items():

                @pl.when(valid & (kind == kd))
                def _():
                    fn(kd, mats, layer)

        def ag_region(j, m, l, flip):
            fixed = {b: bit[b] for b in p.steps[j:]}
            if flip:
                fixed[p.steps[j]] = 1 - bit[p.steps[j]]
            return wreg(m, l, fixed)

        def ag_start(j, m, l):
            reg = ag_region(j, m, l, False)
            to = (s, with_bit(p.steps[j], 1 - bit[p.steps[j]]))
            remote(reg, reg, n.ag_s.at[j, m, l], n.ag_r.at[j, m, l], to).start()

        def ag_wait(j, m, l):
            if j == 0 and m in (OUT, COUT):
                wait(wreg(m, l, mine), n.a2a_r.at[m, l, 0])
            elif j == 0:
                for z in range(tz):
                    fixed = dict(mine)
                    if tz == 2:
                        fixed[PAIR_BIT] = z
                    wait(wreg(m, l, fixed), n.a2a_r.at[m, l, z])
            else:
                wait(ag_region(j - 1, m, l, True), n.ag_r.at[j - 1, m, l])

        def advance(t):
            for j in range(1, nst + 1):

                def fn(kd, mats, l, j=j):
                    for m in mats:
                        ag_wait(j - 1, m, l)
                    for m in mats:
                        ag_start(j - 1, m, l)

                groups(t + nst + 1 - j, fn)

            def last(kd, mats, l):
                for m in mats:
                    ag_wait(nst, m, l)

            groups(t, last)

        @pl.loop(0, nst)
        def _(i):
            advance(i - nst)

        def tp_start(buf, h, st=0):
            mine_rows = buf.at[own]
            for j in range(1, K):
                k2 = rm(k + j, K)
                remote(mine_rows, mine_rows, n.tpa_s.at[st, h, j], n.tpa_r.at[st, h, j], place(core * K + k2, g)).start()
            remote(mine_rows, mine_rows, n.tpa_s.at[st, h, 0], n.tpa_r.at[st, h, 0], sibling).start()

        def tp_finish(buf, h, st=0):
            def rows(c2, k2):
                return buf.at[pl.ds(mul(c2 * K + k2, RR), RR)]

            for j in range(1, K):
                k2 = rm(k - j + K, K)
                ref = rows(core, k2)
                wait(ref, n.tpa_r.at[st, h, j])
                remote(ref, ref, n.tpf_s.at[st, h, j], n.tpf_r.at[st, h, j], sibling).start()
            wait(rows(1 - core, k), n.tpa_r.at[st, h, 0])
            for j in range(1, K):
                wait(rows(1 - core, rm(k - j + K, K)), n.tpf_r.at[st, h, j])
            for j in range(K):
                wait(rows(core, k), n.tpa_s.at[st, h, j])
            for j in range(1, K):
                wait(rows(core, rm(k - j + K, K)), n.tpf_s.at[st, h, j])

        def rs_start(st, h, partial):
            n.rsas[st, h] = partial(mul(1 - core, HB)).astype(bf16)
            copy = remote(n.rsas.at[st, h], n.rsar.at[st, h], n.rsa_s.at[st, h], n.rsa_r.at[st, h], sibling)
            copy.start()
            n.rsp[h] = partial(mul(core, HB))
            wait(n.rsar.at[st, h], n.rsa_r.at[st, h])
            for j in range(1, K):
                k2 = rm(k + j, K)
                rows = pl.ds(mul(k2, RR), RR)
                n.rsbs[st, h, j] = (n.rsp[h, rows] + n.rsar[st, h, rows].astype(f32)).astype(bf16)
                remote(
                    n.rsbs.at[st, h, j],
                    n.rsbr.at[st, h, j],
                    n.rsb_s.at[st, h, j],
                    n.rsb_r.at[st, h, j],
                    place(core * K + k2, g),
                ).start()
            rows = pl.ds(mul(k, RR), RR)
            n.rsp[h, rows] = n.rsp[h, rows] + n.rsar[st, h, rows].astype(f32)
            wait(n.rsas.at[st, h], n.rsa_s.at[st, h])

        def rs_finish(st, h):
            acc = n.rsp[h, pl.ds(mul(k, RR), RR)]
            for j in range(1, K):
                wait(n.rsbr.at[st, h, j], n.rsb_r.at[st, h, j])
                acc = acc + n.rsbr[st, h, j].astype(f32)
            for j in range(1, K):
                wait(n.rsbs.at[st, h, j], n.rsb_s.at[st, h, j])
            return acc

        def halves(fn):
            if NH == 1:
                fn(0)
            else:
                pl.loop(0, NH)(fn)

        def weight(m, l, lo=0, hi=None):
            hi = mat_block[m][1] if hi is None else hi
            at = (l - half if m in DECODER_MATS else l,) + (slice(None),) * (NB + 1) + (slice(lo, hi),)
            return W[m][at].reshape((-1, hi - lo))

        def out_weight(m, l, c):
            parts = [W[m][(l - half if m in DECODER_MATS else l,) + group_bits(m, a * C + c)] for a in range(q)]
            return parts[0] if q == 1 else jnp.concatenate(parts, axis=0)

        def out_product(rows, m, l):
            return jnp.concatenate([dot(rows, out_weight(m, l, c), NN) for c in range(C)], axis=1)

        def out_product_back(grad, m, l):
            acc = None
            for c in range(C):
                term = dot(grad[:, c * cw : (c + 1) * cw], out_weight(m, l, c), NT)
                acc = term if acc is None else acc + term
            return acc

        def norm_row(l, row):
            return n.norms[l][row : row + 1, :]

        def ln_forward(t, h, value, gain, bias):
            centre = value - jnp.mean(value, axis=-1, keepdims=True)
            scale = lax.rsqrt(jnp.mean(centre * centre, axis=-1, keepdims=True) + EPSILON)
            z = centre * scale
            n.zs[t, h] = z.astype(bf16)
            n.rstd[t, h] = jnp.broadcast_to(scale, (RR, 128))
            return z * gain + bias

        def ln_backward(t, h, grad, l, gain_row, bias_row):
            z = n.zs[t, h].astype(f32)
            scale = n.rstd[t, h][:, :1]
            n.small[l, gain_row : gain_row + 1, :] += jnp.sum(grad * z, axis=0, keepdims=True)
            n.small[l, bias_row : bias_row + 1, :] += jnp.sum(grad, axis=0, keepdims=True)
            gz = grad * norm_row(l, gain_row)
            return scale * (
                gz - jnp.mean(gz, axis=-1, keepdims=True) - z * jnp.mean(gz * z, axis=-1, keepdims=True)
            )

        head_width = D // HEADS
        score_scale = 1.0 / math.sqrt(head_width)

        def allowed_of(h, causal):
            rows = lax.broadcasted_iota(jnp.int32, (R, R), 0)
            cols = lax.broadcasted_iota(jnp.int32, (R, R), 1)
            ok = (dv_vec(rows) == dv_vec(cols)) & (n.aux[h][1:2] > 0.5 if causal else n.aux[h][0:1] > 0.5)
            return ok & (cols <= rows) if causal else ok

        def dv_vec(v):
            return lax.div(v, jnp.full_like(v, p.seq))

        def head_lanes(head):
            lane = lax.broadcasted_iota(jnp.int32, (1, CW), 1)
            return (lane >= head * head_width) & (lane < (head + 1) * head_width)

        def only(value, head):
            return jnp.where(head_lanes(head), value, jnp.zeros_like(value))

        def probabilities(qs, ks, allowed, head):
            scores = dot(only(qs, head), ks, NT) * score_scale
            scores = jnp.where(allowed, scores, MASKED)
            e = jnp.exp(scores - jnp.max(scores, axis=-1, keepdims=True))
            return e / jnp.sum(e, axis=-1, keepdims=True)

        def attend(qs, ks, vs, allowed):
            out = jnp.zeros((R, CW), f32)
            for head in range(p.HPR):
                probs = probabilities(qs, ks, allowed, head)
                out = out + only(dot(probs.astype(bf16), vs, NN), head)
            return out.astype(bf16)

        def attend_back(qs, ks, vs, allowed, grad):
            gq = gk = gv = jnp.zeros((R, CW), f32)
            for head in range(p.HPR):
                probs = probabilities(qs, ks, allowed, head)
                gp = dot(only(grad, head), vs, NT)
                gs = (probs * (gp - jnp.sum(gp * probs, axis=-1, keepdims=True))).astype(bf16)
                gv = gv + only(dot(probs.astype(bf16), grad, TN), head)
                gq = gq + only(dot(gs, ks, NN), head)
                gk = gk + only(dot(gs, qs, TN), head)
            return (gq * score_scale).astype(bf16), (gk * score_scale).astype(bf16), gv.astype(bf16)

        def split3(value):
            return value[:, :CW], value[:, CW : 2 * CW], value[:, 2 * CW :]

        c0, c1 = math.sqrt(2.0 / math.pi), 0.044715

        def gelu(v):
            return 0.5 * v * (1.0 + jnp.tanh(c0 * (v + c1 * (v * v * v))))

        def gelu_slope(v):
            th = jnp.tanh(c0 * (v + c1 * (v * v * v)))
            return 0.5 * (1.0 + th) + 0.5 * v * (1.0 - th * th) * (c0 * (1.0 + 3.0 * c1 * v * v))

        def self_forward(l, t, xi, causal, alpha, into):
            advance(t)

            def first(h):
                n.qkv[l, h] = dot(n.xbuf[xi, h], weight(QKV, l), NN).astype(bf16)
                qs, ks, vs = split3(n.qkv[l, h])
                n.osv[l, h] = attend(qs, ks, vs, allowed_of(h, causal))
                rs_start(0, h, lambda row: out_product(n.osv[l, h, pl.ds(row, HB)], OUT, l))

            def second(h):
                value = alpha * n.xbuf[xi, h, own].astype(f32) + rs_finish(0, h)
                hidden = ln_forward(t, h, value, norm_row(l, 0), norm_row(l, 2))
                n.res[h] = hidden
                into[h, own] = hidden.astype(bf16)
                tp_start(into.at[h], h)

            halves(first)
            halves(second)

        def cross_forward(l, t):
            advance(t)
            ld = l - half

            def first(h):
                n.cqkv[ld, h, :, CW:] = dot(n.xbuf[half, h], weight(CQKV, l, CW), NN).astype(bf16)
                tp_finish(n.h1b.at[ld, h], h)
                n.cqkv[ld, h, :, :CW] = dot(n.h1b[ld, h], weight(CQKV, l, 0, CW), NN).astype(bf16)
                qs, ks, vs = split3(n.cqkv[ld, h])
                n.cosv[ld, h] = attend(qs, ks, vs, allowed_of(h, False))
                rs_start(0, h, lambda row: out_product(n.cosv[ld, h, pl.ds(row, HB)], COUT, l))

            def second(h):
                value = DECODER_ALPHA * n.res[h] + rs_finish(0, h)
                hidden = ln_forward(t, h, value, norm_row(l, 4), norm_row(l, 5))
                n.res[h] = hidden
                n.hb[l, h, own] = hidden.astype(bf16)
                tp_start(n.hb.at[l, h], h)

            halves(first)
            halves(second)

        def ffn_forward(l, t, xo, alpha):
            advance(t)

            def first(h):
                tp_finish(n.hb.at[l, h], h)
                before = dot(n.hb[l, h], weight(FIN, l), NN)
                n.pre[l, h] = before.astype(bf16)
                n.act[...] = gelu(before).astype(bf16)
                rs_start(0, h, lambda row: dot(n.act[pl.ds(row, HB)], weight(FOUT, l), NN))

            def second(h):
                value = alpha * n.res[h] + rs_finish(0, h)
                result = ln_forward(t, h, value, norm_row(l, 1), norm_row(l, 3))
                n.xbuf[xo, h, own] = result.astype(bf16)
                tp_start(n.xbuf.at[xo, h], h, 1)

            def third(h):
                tp_finish(n.xbuf.at[xo, h], h, 1)

            halves(first)
            halves(second)
            halves(third)

            @pl.when(s == l)
            def _():
                local(n.xbuf.at[xo, zl], n.out, n.out_l.at[0]).start()

        for i in (2, 0):
            first_wait(i)
        for j in range(1, NS):
            wait(n.norms.at[rm(s - j + NS, NS)], n.norm_r.at[j])
        wait(n.norms.at[s], n.norm_s.at[0])
        n.small[...] = jnp.zeros_like(n.small)
        n.gmem[...] = jnp.zeros_like(n.gmem)

        @pl.loop(0, half)
        def _(l):
            self_forward(l, 2 * l, l, False, ENCODER_ALPHA, n.hb.at[l])
            ffn_forward(l, 2 * l + 1, l + 1, ENCODER_ALPHA)

        for i in (1, 3, 4):
            first_wait(i)

        @pl.loop(half, L)
        def _(l):
            t = 2 * half + 3 * (l - half)
            self_forward(l, t, l + 1, True, DECODER_ALPHA, n.h1b.at[l - half])
            cross_forward(l, t + 1)
            ffn_forward(l, t + 2, l + 2, DECODER_ALPHA)

        def gregion(m, fixed):
            return G[m].at[tuple(fixed.get(b, slice(None)) for b in mat_bits[m])]

        def partner(j):
            b = back_steps[j - 1]
            return (s, with_bit(b, 1 - bit[b]))

        def gr_start(j, kd, mats, l):
            @pl.when(l != L - 1)
            def _():
                pl.semaphore_wait(n.credit.at[j - 1, kd], 1)

            for m in mats:
                fixed = {b: bit[b] for b in back_steps[: j - 1]}
                fixed[back_steps[j - 1]] = 1 - bit[back_steps[j - 1]]
                remote(
                    gregion(m, fixed), RB[m][j], n.gr_s.at[j - 1, m], n.gr_r.at[j - 1, m], partner(j)
                ).start()

        def blocks_of(count):
            return [
                tuple((i >> b) & 1 for b in reversed(range(count))) for i in range(1 << count)
            ]

        def gr_finish(j, kd, mats, l):
            for m in mats:
                wait(RB[m][j], n.gr_r.at[j - 1, m])
                mine_part = gregion(m, {b: bit[b] for b in back_steps[:j]})
                for idx in blocks_of(len(mat_bits[m]) - j):
                    value = mine_part[idx].astype(f32) + RB[m][j][idx].astype(f32)
                    if j == nst:
                        ST[m][idx if idx else 0] = value.astype(bf16)
                    else:
                        mine_part[idx] = value.astype(bf16)
                wait(RB[m][j], n.gr_s.at[j - 1, m])

            @pl.when(l != (half if kd == CROSS else 0))
            def _():
                pl.semaphore_signal(n.credit.at[j - 1, kd], inc=1, device_id=partner(j), device_id_type=MESH)

        def home(m, l, z, act):
            src = ST[m].at[z]
            if m in (OUT, COUT):
                piece = rm(g, C)
                to = (l, r * q + dv(g, C))
                here = (l == s) & (to[1] == d)
                dst, slot = H[m].at[:, pl.ds(mul(piece, cw), cw)], piece
            else:
                to = (l, with_bit(PAIR_BIT, z) if tz == 2 else d)
                here = (l == s) & (zl == z) if tz == 2 else l == s
                dst, slot = H[m].at[r], r

            if act == "wait":
                wait(src, n.home_s.at[m, z])
                return

            @pl.when(here)
            def _():
                local(src, dst, n.home_s.at[m, z]).start()

            @pl.when(jnp.logical_not(here))
            def _():
                remote(src, dst, n.home_s.at[m, z], n.home_r.at[m, slot], to).start()

        def process(u):
            def old(kd, mats, l):
                for m in mats:
                    for z in range(ST[m].shape[0]):
                        home(m, l, z, "wait")

            groups(T - 1 - (u - nst - 1), old)
            for j in range(nst, 0, -1):

                def fn(kd, mats, l, j=j):
                    gr_finish(j, kd, mats, l)
                    if j < nst:
                        gr_start(j + 1, kd, mats, l)
                    else:
                        for m in mats:
                            for z in range(ST[m].shape[0]):
                                home(m, l, z, "start")

                groups(T - 1 - (u - j), fn)

        def weight_grad(m, lefts, rights):
            rows, cols = mat_block[m]
            count = max(1, 128 // rows)
            tile = rows * count

            @pl.loop(0, ND // count)
            def _(i):
                span = pl.ds(mul(i, tile), tile)
                parts = []
                for left, right in zip(lefts, rights):
                    acc = None
                    for h in range(NH):
                        term = dot(left[h][:, span], right[h][...], TN)
                        acc = term if acc is None else acc + term
                    parts.append(acc)
                value = parts[0] if len(parts) == 1 else jnp.concatenate(parts, axis=1)
                value = value.astype(bf16)
                for e in range(count):
                    at = i * count + e
                    idx = tuple(rm(dv(at, 1 << b), 2) for b in reversed(range(NB)))
                    G[m][idx] = value[e * rows : (e + 1) * rows]

        def out_grad(m, left, right):
            for c in range(C):
                acc = None
                for h in range(NH):
                    term = dot(left[h][...], right[h][:, c * cw : (c + 1) * cw], TN)
                    acc = term if acc is None else acc + term
                acc = acc.astype(bf16)
                for a in range(q):
                    G[m][group_bits(m, a * C + c)] = acc[a * p.rb : (a + 1) * p.rb]

        def each(ref):
            return [ref.at[h] for h in range(NH)]

        def branch_grad(t, l, u, gain_row, bias_row):
            gag = n.gag.at[rm(u, 2)]

            def fn(h):
                grad = ln_backward(t, h, n.gy[h], l, gain_row, bias_row)
                n.res[h] = grad
                gag[h, own] = grad.astype(bf16)
                tp_start(gag.at[h], h)

            halves(fn)
            return gag

        def ffn_backward(l, t, u, alpha):
            gag = branch_grad(t, l, u, 1, 3)

            def first(h):
                tp_finish(gag.at[h], h)
                before = n.pre[l, h].astype(f32)
                gact = dot(gag[h], weight(FOUT, l), NT)
                n.gpre[h] = (gact * gelu_slope(before)).astype(bf16)
                rs_start(0, h, lambda row: dot(n.gpre[h, pl.ds(row, HB)], weight(FIN, l), NT))
                n.actb[h] = gelu(before).astype(bf16)

            halves(first)
            process(u)
            weight_grad(FOUT, [each(n.actb)], [each(gag)])
            weight_grad(FIN, [each(n.hb.at[l])], [each(n.gpre)])
            gr_start(1, FFN, KIND_MATS[FFN], l)

            def second(h):
                n.gy[h] = alpha * n.res[h] + rs_finish(0, h)

            halves(second)

        def cross_backward(l, t, u):
            gag = branch_grad(t, l, u, 4, 5)
            ld = l - half

            def first(h):
                tp_finish(gag.at[h], h)
                grad = out_product_back(gag.at[h], COUT, l).astype(bf16)
                qs, ks, vs = split3(n.cqkv[ld, h])
                gq, gk, gv = attend_back(qs, ks, vs, allowed_of(h, False), grad)
                n.gqkv[h, :, :CW] = gq
                n.gqkv[h, :, CW : 2 * CW] = gk
                n.gqkv[h, :, 2 * CW :] = gv
                rs_start(
                    0, h, lambda row: dot(n.gqkv[h, pl.ds(row, HB), :CW], weight(CQKV, l, 0, CW), NT)
                )
                n.gmem[h] += dot(n.gqkv[h, :, CW:], weight(CQKV, l, CW), NT)

            halves(first)
            process(u)
            out_grad(COUT, each(n.cosv.at[ld]), each(gag))
            weight_grad(
                CQKV,
                [each(n.h1b.at[ld]), each(n.xbuf.at[half])],
                [
                    [n.gqkv.at[h, :, pl.ds(0, CW)] for h in range(NH)],
                    [n.gqkv.at[h, :, pl.ds(CW, 2 * CW)] for h in range(NH)],
                ],
            )
            gr_start(1, CROSS, KIND_MATS[CROSS], l)

            def second(h):
                n.gy[h] = DECODER_ALPHA * n.res[h] + rs_finish(0, h)

            halves(second)

        def sig_copy(l, h, act):
            here = (l == s) & (h == zl)
            src = n.gxo.at[l, h]

            @pl.when(here)
            def _():
                if act == "start":
                    local(src, n.sig.at[own], n.sig_r.at[r]).start()

            @pl.when(jnp.logical_not(here))
            def _():
                if act == "start":
                    to = (l, with_bit(PAIR_BIT, h) if tz == 2 else d)
                    remote(src, n.sig.at[own], n.sig_s.at[l, h], n.sig_r.at[r], to).start()
                else:
                    wait(src, n.sig_s.at[l, h])

        def self_backward(l, t, u, xi, causal, alpha):
            gag = branch_grad(t, l, u, 0, 2)

            def first(h):
                tp_finish(gag.at[h], h)
                grad = out_product_back(gag.at[h], OUT, l).astype(bf16)
                qs, ks, vs = split3(n.qkv[l, h])
                gq, gk, gv = attend_back(qs, ks, vs, allowed_of(h, causal), grad)
                n.gqkv[h, :, :CW] = gq
                n.gqkv[h, :, CW : 2 * CW] = gk
                n.gqkv[h, :, 2 * CW :] = gv
                rs_start(0, h, lambda row: dot(n.gqkv[h, pl.ds(row, HB)], weight(QKV, l), NT))

            halves(first)
            process(u)
            out_grad(OUT, each(n.osv.at[l]), each(gag))
            weight_grad(QKV, [each(n.xbuf.at[xi])], [each(n.gqkv)])
            gr_start(1, ATTN, KIND_MATS[ATTN], l)

            def second(h):
                grad = (alpha * n.res[h] + rs_finish(0, h)).astype(bf16)
                n.gxo[l, h] = grad
                n.gy[h] = grad.astype(f32)
                sig_copy(l, h, "start")

            halves(second)

        def seed(h):
            n.gy[h] = n.cotb[h].astype(f32)

        halves(seed)

        @pl.loop(0, LD)
        def _(i):
            l = L - 1 - i
            t = 2 * half + 3 * (l - half)
            ffn_backward(l, t + 2, 3 * i, DECODER_ALPHA)
            cross_backward(l, t + 1, 3 * i + 1)
            self_backward(l, t, 3 * i + 2, l + 1, True, DECODER_ALPHA)

        def directions(h):
            column = n.dirw[h, dv(r * RR, p.seq)][:, :1]
            rows = column * jnp.sum(n.gy[h], axis=0, keepdims=True)
            for sec in range(NS):
                lo = sec * p.dir_rows
                n.small[sec, 8 : 8 + p.dir_rows, :] += rows[lo : lo + p.dir_rows]

        halves(directions)

        def memory_first(h):
            rs_start(1, h, lambda row: n.gmem[h, pl.ds(row, HB)])

        def memory_second(h):
            n.gy[h] = rs_finish(1, h).astype(bf16).astype(f32)

        halves(memory_first)
        halves(memory_second)

        @pl.loop(0, half)
        def _(i):
            l = half - 1 - i
            u = 3 * LD + 2 * i
            ffn_backward(l, 2 * l + 1, u, ENCODER_ALPHA)
            self_backward(l, 2 * l, u + 1, l, False, ENCODER_ALPHA)

        for rank in range(TPN):
            for g2 in range(NU):
                sec, d2 = place(rank, g2)
                lo = d2 * p.cols
                tile, lane = divmod(g2 * p.cols, 128)
                n.sm1[rank, tile, :, lane : lane + p.cols] = n.small[sec, :, lo : lo + p.cols]
        for j in range(1, TPN):
            to = rm(r + j, TPN)
            remote(n.sm1.at[to], n.sm1r.at[j], n.sm1_s.at[j], n.sm1_rs.at[j], place(to, g)).start()

        @pl.loop(0, nst + 1)
        def _(i):
            process(T + i)

        total_small = n.sm1[r]
        for j in range(1, TPN):
            wait(n.sm1r.at[j], n.sm1_rs.at[j])
            total_small = total_small + n.sm1r[j]
        for g2 in range(NU):
            tile, lane = divmod(g2 * p.cols, 128)
            n.sm2[g2, :, : p.cols] = total_small[tile, :, lane : lane + p.cols]
        for j in range(1, NU):
            to = rm(g + j, NU)
            remote(n.sm2.at[to], n.sm2r.at[j], n.sm2_s.at[j], n.sm2_rs.at[j], place(r, to)).start()
        mine_small = n.sm2[g]
        for j in range(1, NU):
            wait(n.sm2r.at[j], n.sm2_rs.at[j])
            mine_small = mine_small + n.sm2r[j]
        n.smo[...] = mine_small
        local(n.smo, n.smout, n.smo_l.at[0]).start()
        wait(n.smo, n.smo_l.at[0])

        def home_wait(m):
            for j in range(1, TPN):
                rank = rm(r + j, TPN)
                wait(H[m].at[rank], n.home_r.at[m, rank])

        def home_wait_out(m):
            for c, span, group, rank, here in out_pieces(m):

                @pl.when(jnp.logical_not(here))
                def _():
                    wait(H[m].at[:, span], n.home_r.at[m, c])

        for m in (QKV, FIN, FOUT):
            home_wait(m)
        home_wait_out(OUT)

        @pl.when(s >= half)
        def _():
            home_wait(CQKV)
            home_wait_out(COUT)

        for rank in range(TPN):
            wait(n.sig.at[pl.ds(rank * RR, RR)], n.sig_r.at[rank])
        wait(n.out, n.out_l.at[0])
        for l in range(L):
            for h in range(NH):
                sig_copy(l, h, "wait")
        for j in range(1, TPN):
            wait(n.sm1.at[0], n.sm1_s.at[j])
        for j in range(1, NU):
            wait(n.sm2.at[0], n.sm2_s.at[j])
        for j in range(1, NS):
            wait(n.norms.at[0], n.norm_s.at[j])
        for j in range(1, TPN):
            for m in (QKV, FIN, FOUT):
                wait(A[m].at[0], n.a2a_s.at[m, j])

        @pl.when(s >= half)
        def _():
            for j in range(1, TPN):
                wait(A[CQKV].at[0], n.a2a_s.at[CQKV, j])

        for m in (OUT, COUT):
            for c, span, group, rank, here in out_pieces(m):
                sends = jnp.logical_not(here) if m == OUT else jnp.logical_not(here) & (s >= half)

                @pl.when(sends)
                def _():
                    wait(n.woi.at[:, span], n.wo_s.at[m - OUT, c])

        @pl.loop(0, L)
        def _(l):
            for j in range(nst):
                for m in mat_block:
                    if m not in DECODER_MATS:
                        wait(ag_region(j, m, l, False), n.ag_s.at[j, m, l])

                @pl.when(l >= half)
                def _():
                    for m in DECODER_MATS:
                        wait(ag_region(j, m, l, False), n.ag_s.at[j, m, l])

    def sd(*shape, dtype=bf16):
        return jax.ShapeDtypeStruct(shape, dtype)

    def blocks(m, lead):
        return sd(lead, *mat_block[m])

    outs = [
        sd(R, D),
        sd(R, D),
        blocks(QKV, TPN),
        blocks(FIN, TPN),
        blocks(FOUT, TPN),
        blocks(CQKV, TPN),
        sd(p.rb, D),
        sd(p.rb, D),
        sd(16, 128, dtype=f32),
    ]
    anywhere = pl.BlockSpec(memory_space=pl.ANY)
    return pl.pallas_call(
        kernel,
        out_shape=outs,
        in_specs=[anywhere] * len(in_names),
        out_specs=[anywhere] * len(out_names),
        scratch_shapes=list(scratch.values()),
        compiler_params=pltpu.CompilerParams(
            collective_id=0, has_side_effects=True, vmem_limit_bytes=64 * 1024 * 1024 - 64 * 1024
        ),
    )


def solution(mesh):
    def body(
        source,
        target,
        directions,
        source_lengths,
        target_lengths,
        attn_in,
        attn_out,
        ffn_in,
        ffn_out,
        cross_weight,
        norm_gain,
        norm_bias,
        cross_norm,
        dir_table,
        cotangent,
    ):
        pairs, seq, width = source.shape
        p = make_plan(
            mesh.shape["section"], mesh.shape["dp"], pairs, seq, width, ffn_in.shape[2], dir_table.shape[0]
        )
        section = lax.axis_index("section")
        routing = (directions[:, None] == jnp.arange(p.NDIR)[None, :]).astype(f32)
        rows = jnp.dot(routing, dir_table, precision=lax.Precision.HIGHEST)
        x2 = (target.astype(f32) + rows[:, None, :]).astype(bf16).reshape(p.R, width)
        positions = jnp.arange(seq)
        valid = [(positions[None, :] < lens[:, None]).astype(f32).reshape(1, p.R) for lens in (source_lengths, target_lengths)]
        aux = jnp.concatenate(valid + [jnp.zeros((6, p.R), f32)], axis=0)
        dirw = jnp.broadcast_to(routing[:, :, None], (pairs, p.NDIR, 128))
        norms = jnp.concatenate(
            (norm_gain[0], norm_bias[0], cross_norm[0], jnp.zeros((2, width), bf16)), axis=0
        ).astype(f32)
        aq = attn_in[0].reshape(p.rb, 3, p.TPN, p.CW).transpose(2, 0, 1, 3).reshape(p.TPN, p.rb, 3 * p.CW)
        cross = cross_weight[0][:, : 3 * width]
        ac = cross.reshape(p.rb, 3, p.TPN, p.CW).transpose(2, 0, 1, 3).reshape(p.TPN, p.rb, 3 * p.CW)
        ai = ffn_in[0].reshape(p.rb, p.ND, p.TPN, p.fb).transpose(2, 0, 1, 3).reshape(p.TPN, p.rb, p.FB)
        af = ffn_out[0].reshape(p.TPN, p.fb, width)
        out, sig, hq, hi, hf, hc, hwo, hwco, small = build(p)(
            source.reshape(p.R, width),
            x2,
            cotangent.reshape(p.R, width),
            aux,
            dirw,
            norms,
            aq,
            ai,
            af,
            ac,
            attn_out[0],
            cross_weight[0][:, 3 * width :],
        )
        decoder = section >= p.half

        def heads_back(value):
            value = value.reshape(p.TPN, p.rb, 3, p.CW).transpose(1, 2, 0, 3)
            return value.reshape(1, p.rb, 3 * width).astype(f32)

        g_in = hi.reshape(p.TPN, p.rb, p.ND, p.fb).transpose(1, 2, 0, 3).reshape(1, p.rb, p.FF).astype(f32)
        g_out = hf.reshape(1, p.TPN * p.fb, width).astype(f32)
        g_wo = hwo.astype(f32)[None]
        g_cross = jnp.concatenate((heads_back(hc), hwco.astype(f32)[None]), axis=2)
        g_cross = jnp.where(decoder, g_cross, jnp.zeros_like(g_cross))
        small = small[:, : p.cols]
        return (
            out.reshape(1, pairs, seq, width),
            sig.reshape(1, pairs, seq, width),
            heads_back(hq),
            g_wo,
            g_in,
            g_out,
            g_cross,
            small[None, 0:2],
            small[None, 2:4],
            small[None, 4:6],
            small[8 : 8 + p.dir_rows],
        )

    sharded = P("section", "dp", None)
    return jax.shard_map(
        body,
        mesh=mesh,
        in_specs=(
            P("dp", None, None),
            P("dp", None, None),
            P("dp"),
            P("dp"),
            P("dp"),
            sharded,
            sharded,
            sharded,
            sharded,
            sharded,
            P("section", None, None),
            P("section", None, None),
            P("section", None, None),
            P(),
            P("dp", None, None),
        ),
        out_specs=(
            P("section", "dp", None, None),
            P("section", "dp", None, None),
            sharded,
            sharded,
            sharded,
            sharded,
            sharded,
            P("section", None, "dp"),
            P("section", None, "dp"),
            P("section", None, "dp"),
            P("section", "dp"),
        ),
        check_vma=False,
    )
```

time: 3380 us -> 676 us (0.20)
  waiting for transfers between devices: 2520 us -> 0 us
  Pallas kernels: 0 us -> 647 us
  matrix products: 365 us -> 0.2 us
  local copies, waits for them, and re-layouts: 204 us -> 22.8 us
  other arithmetic: 155 us -> 5.03 us
  loops' own time: 71 us -> 0 us
  starting transfers between devices: 35.9 us -> 0 us
    psum x14 -> x0, waiting for transfers between devices: 1160 us -> none  [the longest x7 852 us: backward_clock(): lax.psum(pick_row(memory_parts, slot_index).astype(jnp.bfloat16), 'section')]
    pallas_call x0 -> x1, Pallas kernels: none -> 647 us  [body(): build(p)]
    reduce_scatter x5 -> x0, waiting for transfers between devices: 637 us -> none  [the longest x1 149 us: body(): lax.psum_scatter(totals[3].astype(jnp.bfloat16), 'dp', scatter_dimension=...]
    all_gather x5 -> x0, waiting for transfers between devices: 523 us -> none  [the longest x1 125 us: body(): lax.all_gather(ffn_in, 'dp', axis=1, tiled=True)]
    dot_general x89 -> x1, matrix products: 359 us -> 0.2 us  [body(): rows = jnp.dot(routing, dir_table, precision=lax.Precision.HIGHEST)]
    unnamed x16 -> x0, waiting for transfers between devices: 203 us -> none
    another operation x16 -> x0, loops' own time: 71 us -> none  [the longest x7 47.2 us: backward_clock(): lax.switch(branch_index, [skip_backward, backward_encoder_branch, backwar...]
    dynamic_update_slice x42 -> x0, other arithmetic: 63.6 us -> none  [put_row(): lax.dynamic_update_index_in_dim(array, jnp.where(active, value, pick_row(...]
  transfers between devices with their start and end apart: 41 -> 0, of which waited for: 27 -> 0; matrix products, arithmetic and copies ran while one was open for 5% -> 0% of each run, Pallas kernels for 0% -> 0%
where the time goes in v1:
time: 676 us
  Pallas kernels  647 us (96%)
  local copies, waits for them, and re-layouts  22.8 us (3%)
    pallas_call x1, Pallas kernels, body(): build(p)  647 us

profile of v1, /device:TPU:0, one launch (start us, length us, event | category | flops | bytes accessed | tf_op | source)
XLA Modules:
  0.0 676.1 jit_solution(4325134760740983383)
XLA Ops:
  0.6 1.2 slice_bitcast_fusion
  1.8 0.2 copy.61
  2.0 0.0 copy-start.2
  2.0 0.6 copy.47
  2.6 1.2 copy.50.refs_9_
  3.7 1.7 slice.25.refs_11_
  5.4 0.0 copy-done.2
  5.4 0.7 copy.45
  6.1 0.0 copy-start.3
  6.1 0.1 copy.46
  6.2 1.3 copy.49.refs_7_
  7.5 0.0 copy-done.3
  7.5 0.4 copy.43
  7.9 0.0 copy-start.11
  7.9 0.0 copy-start.12
  7.9 0.0 copy-start.13
  7.9 0.0 copy-start.16
  7.9 0.0 copy-start.17
  7.9 0.1 copy.44
  8.0 1.2 copy.48.refs_6_
  9.2 0.0 copy-done.10
  9.2 0.0 copy-done.15
  9.2 0.2 fusion.1
  9.4 0.0 copy-done.5
  9.4 0.9 add_convert_fusion
  10.3 0.1 fusion
  10.4 0.7 broadcast_in_dim.39.refs_4_
  11.1 0.1 pad.5.clone
  11.2 0.0 copy-done.11
  11.2 0.0 copy-done.12
  11.2 0.0 copy-done.13
  11.2 0.7 maximum_convert_fusion.refs_5_
  11.9 0.0 copy-done.16
  11.9 0.1 fusion.2
  11.9 0.1 reshape.235
  12.0 0.0 copy-done.17
  12.0 0.1 fusion.3
  12.1 0.1 reshape.236
  12.2 0.1 pad.8.clone
  12.3 0.7 maximum_maximum_fusion.refs_3_
  12.9 647.2 %shard_map.230 = (bf16[256,1024]{1,0:T(8,128)(2,1)}, bf16[256,1024]{1,0:T(8,128)(2,1)}, bf16[8,128,384]{2,1,0:T(8,128)(2,1)}, bf16[8,128,512]{2,1,0:T(8,128)(2,1...) custom-call(bf16[256,1024]{1,0:T(8,128)(2,1)} %bitcast.70, ...), custom_call_target="tpu_custom_call" | custom-call | tf_op jit(solution)/shard_map/pallas_call | solution.py:1039
  660.1 0.0 copy-start.9
  660.1 1.5 copy.55
  661.7 0.1 copy.56
  661.8 0.0 copy-done.9
  661.8 0.2 copy.57
  662.0 0.1 convert_select_fusion
  662.1 0.0 copy-start.14
  662.1 1.8 copy.60
  663.9 0.6 slice_bitcast_fusion.1
  664.5 0.6 slice.23
  665.1 0.0 copy-done.1
  665.1 0.5 copy.53
  665.6 1.5 copy.54
  667.1 3.0 copy.59
  670.0 0.3 copy.51
  670.3 0.1 copy.52
  670.5 0.0 copy-start
  670.5 1.6 copy.58
  672.1 1.6 bitcast_convert_fusion
  673.7 0.8 bitcast_convert_fusion.1
  674.5 0.0 copy-done.7
  674.5 0.8 copy.64
  675.3 0.8 copy.65
  (15 shorter events, 0.0 us)
Async XLA Ops:
  2.0 3.4 copy-start.2
  6.1 1.4 copy-start.3
  7.5 1.7 copy-start.10
  7.5 1.7 copy-start.15
  7.5 1.9 copy-start.5
  7.9 3.3 copy-start.11
  7.9 3.3 copy-start.12
  7.9 3.3 copy-start.13
  7.9 3.9 copy-start.16
  7.9 4.1 copy-start.17
  660.1 1.6 copy-start.9
  662.1 1.8 copy-start.14
  662.1 3.0 copy-start.1
  667.1 3.0 copy-start.4
  670.5 1.6 copy-start
  672.1 1.6 copy-start.8
  672.1 2.4 copy-start.7
  672.1 3.2 copy-start.6

commit v2 on v1

--- a/solution.py
+++ b/solution.py
@@ -10,7 +10,9 @@
 
 HEADS = 16
 GROUP = 8
-PAIR_BIT = 1
+AHEAD = (4, 3, 2)
+BEHIND = (2, 3)
+PAIR_BIT = 0
 ENCODER_ALPHA = 3.42
 DECODER_ALPHA = 4.16
 MASKED = -1000000000.0
@@ -157,9 +159,10 @@
         out_l=dma((L,)),
         smo_l=dma((1,)),
     )
+    slots = 2 if nst == 2 else 1
     for m, block in mat_block.items():
         scratch["w%d" % m] = vm((LD if m in DECODER_MATS else L,) + two[m] + block, bf16)
-        scratch["g%d" % m] = vm(two[m] + block, bf16)
+        scratch["g%d" % m] = vm((slots,) + two[m] + block, bf16)
         scratch["st%d" % m] = vm((2 ** (len(two[m]) - nst),) + block, bf16)
         for j in range(1, nst + 1):
             scratch["r%d_%d" % (m, j)] = vm(two[m][j:] + block, bf16)
@@ -181,12 +184,13 @@
         zl = bit[PAIR_BIT] if tz == 2 else 0
         k = zl * (NS // 2) + x
         r = core * K + k
-        g = dv(d, 4) * 2 + rm(d, 2) if tz == 2 else d
+        low = 1 << PAIR_BIT
+        g = dv(d, 2 * low) * low + rm(d, low) if tz == 2 else d
 
         def place(rank, group):
             c2, k2 = dv(rank, K), rm(rank, K)
             x2, z2 = rm(k2, NS // 2), dv(k2, NS // 2)
-            d2 = dv(group, 2) * 4 + z2 * 2 + rm(group, 2) if tz == 2 else group
+            d2 = dv(group, low) * 2 * low + z2 * low + rm(group, low) if tz == 2 else group
             return (x2 * 2 + c2, d2)
 
         def with_bit(b, value):
@@ -283,20 +287,6 @@
                 def _():
                     remote(src.at[:, span], dst, n.wo_s.at[m - OUT, c], n.a2a_r.at[m, s, 0], place(rank, group)).start()
 
-        a2a_start(QKV)
-        out_start(OUT, n.woi)
-        a2a_start(FIN)
-        a2a_start(FOUT)
-
-        @pl.when(s >= half)
-        def _():
-            a2a_start(CQKV)
-            out_start(COUT, n.wcoi)
-
-        first_start(1)
-        first_start(4)
-        first_start(3)
-
         def kind_layer(t):
             td = jnp.maximum(t - 2 * half, 0)
             is_enc = t < 2 * half
@@ -337,7 +327,21 @@
             else:
                 wait(ag_region(j - 1, m, l, True), n.ag_r.at[j - 1, m, l])
 
-        def advance(t):
+        ahead = AHEAD if nst == 2 else tuple(range(nst + 1, 0, -1))
+
+        def feed(t):
+            def fn0(kd, mats, l):
+                @pl.when(l == s)
+                def _():
+                    for m in mats:
+                        if m == OUT:
+                            out_start(OUT, n.woi)
+                        elif m == COUT:
+                            out_start(COUT, n.wcoi)
+                        else:
+                            a2a_start(m)
+
+            groups(t + ahead[0], fn0)
             for j in range(1, nst + 1):
 
                 def fn(kd, mats, l, j=j):
@@ -346,17 +350,22 @@
                     for m in mats:
                         ag_start(j - 1, m, l)
 
-                groups(t + nst + 1 - j, fn)
-
+                groups(t + ahead[j], fn)
+
+        def ready(t):
             def last(kd, mats, l):
                 for m in mats:
                     ag_wait(nst, m, l)
 
             groups(t, last)
 
-        @pl.loop(0, nst)
+        @pl.loop(0, ahead[0])
         def _(i):
-            advance(i - nst)
+            feed(i - ahead[0])
+
+        first_start(1)
+        first_start(4)
+        first_start(3)
 
         def tp_start(buf, h, st=0):
             mine_rows = buf.at[own]
@@ -514,7 +523,8 @@
             return 0.5 * (1.0 + th) + 0.5 * v * (1.0 - th * th) * (c0 * (1.0 + 3.0 * c1 * v * v))
 
         def self_forward(l, t, xi, causal, alpha, into):
-            advance(t)
+            feed(t)
+            ready(t)
 
             def first(h):
                 n.qkv[l, h] = dot(n.xbuf[xi, h], weight(QKV, l), NN).astype(bf16)
@@ -533,7 +543,8 @@
             halves(second)
 
         def cross_forward(l, t):
-            advance(t)
+            feed(t)
+            ready(t)
             ld = l - half
 
             def first(h):
@@ -555,7 +566,8 @@
             halves(second)
 
         def ffn_forward(l, t, xo, alpha):
-            advance(t)
+            feed(t)
+            ready(t)
 
             def first(h):
                 tp_finish(n.hb.at[l, h], h)
@@ -604,8 +616,11 @@
             cross_forward(l, t + 1)
             ffn_forward(l, t + 2, l + 2, DECODER_ALPHA)
 
-        def gregion(m, fixed):
-            return G[m].at[tuple(fixed.get(b, slice(None)) for b in mat_bits[m])]
+        def gbuf(m, l):
+            return G[m].at[rm(l, slots)]
+
+        def gregion(m, l, fixed):
+            return gbuf(m, l).at[tuple(fixed.get(b, slice(None)) for b in mat_bits[m])]
 
         def partner(j):
             b = back_steps[j - 1]
@@ -620,7 +635,7 @@
                 fixed = {b: bit[b] for b in back_steps[: j - 1]}
                 fixed[back_steps[j - 1]] = 1 - bit[back_steps[j - 1]]
                 remote(
-                    gregion(m, fixed), RB[m][j], n.gr_s.at[j - 1, m], n.gr_r.at[j - 1, m], partner(j)
+                    gregion(m, l, fixed), RB[m][j], n.gr_s.at[j - 1, m], n.gr_r.at[j - 1, m], partner(j)
                 ).start()
 
         def blocks_of(count):
@@ -631,7 +646,7 @@
         def gr_finish(j, kd, mats, l):
             for m in mats:
                 wait(RB[m][j], n.gr_r.at[j - 1, m])
-                mine_part = gregion(m, {b: bit[b] for b in back_steps[:j]})
+                mine_part = gregion(m, l, {b: bit[b] for b in back_steps[:j]})
                 for idx in blocks_of(len(mat_bits[m]) - j):
                     value = mine_part[idx].astype(f32) + RB[m][j][idx].astype(f32)
                     if j == nst:
@@ -668,13 +683,15 @@
             def _():
                 remote(src, dst, n.home_s.at[m, z], n.home_r.at[m, slot], to).start()
 
+        behind = BEHIND if nst == 2 else tuple(range(1, nst + 1))
+
         def process(u):
             def old(kd, mats, l):
                 for m in mats:
                     for z in range(ST[m].shape[0]):
                         home(m, l, z, "wait")
 
-            groups(T - 1 - (u - nst - 1), old)
+            groups(T - 1 - (u - behind[nst - 1] - 1), old)
             for j in range(nst, 0, -1):
 
                 def fn(kd, mats, l, j=j):
@@ -686,9 +703,9 @@
                             for z in range(ST[m].shape[0]):
                                 home(m, l, z, "start")
 
-                groups(T - 1 - (u - j), fn)
-
-        def weight_grad(m, lefts, rights):
+                groups(T - 1 - (u - behind[j - 1]), fn)
+
+        def weight_grad(m, l, lefts, rights):
             rows, cols = mat_block[m]
             count = max(1, 128 // rows)
             tile = rows * count
@@ -708,9 +725,9 @@
                 for e in range(count):
                     at = i * count + e
                     idx = tuple(rm(dv(at, 1 << b), 2) for b in reversed(range(NB)))
-                    G[m][idx] = value[e * rows : (e + 1) * rows]
-
-        def out_grad(m, left, right):
+                    gbuf(m, l)[idx] = value[e * rows : (e + 1) * rows]
+
+        def out_grad(m, l, left, right):
             for c in range(C):
                 acc = None
                 for h in range(NH):
@@ -718,7 +735,7 @@
                     acc = term if acc is None else acc + term
                 acc = acc.astype(bf16)
                 for a in range(q):
-                    G[m][group_bits(m, a * C + c)] = acc[a * p.rb : (a + 1) * p.rb]
+                    gbuf(m, l)[group_bits(m, a * C + c)] = acc[a * p.rb : (a + 1) * p.rb]
 
         def each(ref):
             return [ref.at[h] for h in range(NH)]
@@ -748,8 +765,8 @@
 
             halves(first)
             process(u)
-            weight_grad(FOUT, [each(n.actb)], [each(gag)])
-            weight_grad(FIN, [each(n.hb.at[l])], [each(n.gpre)])
+            weight_grad(FOUT, l, [each(n.actb)], [each(gag)])
+            weight_grad(FIN, l, [each(n.hb.at[l])], [each(n.gpre)])
             gr_start(1, FFN, KIND_MATS[FFN], l)
 
             def second(h):
@@ -776,9 +793,10 @@
 
             halves(first)
             process(u)
-            out_grad(COUT, each(n.cosv.at[ld]), each(gag))
+            out_grad(COUT, l, each(n.cosv.at[ld]), each(gag))
             weight_grad(
                 CQKV,
+                l,
                 [each(n.h1b.at[ld]), each(n.xbuf.at[half])],
                 [
                     [n.gqkv.at[h, :, pl.ds(0, CW)] for h in range(NH)],
@@ -824,8 +842,8 @@
 
             halves(first)
             process(u)
-            out_grad(OUT, each(n.osv.at[l]), each(gag))
-            weight_grad(QKV, [each(n.xbuf.at[xi])], [each(n.gqkv)])
+            out_grad(OUT, l, each(n.osv.at[l]), each(gag))
+            weight_grad(QKV, l, [each(n.xbuf.at[xi])], [each(n.gqkv)])
             gr_start(1, ATTN, KIND_MATS[ATTN], l)
 
             def second(h):
@@ -884,7 +902,7 @@
             to = rm(r + j, TPN)
             remote(n.sm1.at[to], n.sm1r.at[j], n.sm1_s.at[j], n.sm1_rs.at[j], place(to, g)).start()
 
-        @pl.loop(0, nst + 1)
+        @pl.loop(0, behind[nst - 1] + 1)
         def _(i):
             process(T + i)
 

time: 676 us -> 621 us (0.919)
  Pallas kernels: 647 us -> 592 us
    pallas_call x1, Pallas kernels: 647 us -> 592 us  [body(): build(p)]
where the time goes in v2:
time: 621 us
  Pallas kernels  592 us (95%)
  local copies, waits for them, and re-layouts  22.8 us (4%)
    pallas_call x1, Pallas kernels, body(): build(p)  592 us

profile of v2, /device:TPU:0, one launch (start us, length us, event | category | flops | bytes accessed | tf_op | source)
XLA Modules:
  0.0 620.6 jit_solution(12243024525885957686)
XLA Ops:
  0.6 1.2 slice_bitcast_fusion
  1.8 0.2 copy.61
  2.0 0.0 copy-start.2
  2.0 0.6 copy.47
  2.6 1.2 copy.50.refs_9_
  3.7 1.7 slice.25.refs_11_
  5.4 0.0 copy-done.2
  5.4 0.7 copy.45
  6.1 0.0 copy-start.3
  6.1 0.1 copy.46
  6.2 1.3 copy.49.refs_7_
  7.5 0.0 copy-done.3
  7.5 0.4 copy.43
  7.9 0.0 copy-start.11
  7.9 0.0 copy-start.12
  7.9 0.0 copy-start.13
  7.9 0.0 copy-start.16
  7.9 0.0 copy-start.17
  7.9 0.1 copy.44
  8.0 1.2 copy.48.refs_6_
  9.2 0.0 copy-done.10
  9.2 0.0 copy-done.15
  9.2 0.2 fusion.1
  9.4 0.0 copy-done.5
  9.4 0.9 add_convert_fusion
  10.3 0.1 fusion
  10.4 0.7 broadcast_in_dim.39.refs_4_
  11.1 0.1 pad.5.clone
  11.2 0.0 copy-done.11
  11.2 0.0 copy-done.12
  11.2 0.0 copy-done.13
  11.2 0.7 maximum_convert_fusion.refs_5_
  11.9 0.0 copy-done.16
  11.9 0.1 fusion.2
  11.9 0.1 reshape.235
  12.0 0.0 copy-done.17
  12.0 0.1 fusion.3
  12.1 0.1 reshape.236
  12.2 0.1 pad.8.clone
  12.3 0.7 maximum_maximum_fusion.refs_3_
  12.9 591.7 %shard_map.230 = (bf16[256,1024]{1,0:T(8,128)(2,1)}, bf16[256,1024]{1,0:T(8,128)(2,1)}, bf16[8,128,384]{2,1,0:T(8,128)(2,1)}, bf16[8,128,512]{2,1,0:T(8,128)(2,1...) custom-call(bf16[256,1024]{1,0:T(8,128)(2,1)} %bitcast.70, ...), custom_call_target="tpu_custom_call" | custom-call | tf_op jit(solution)/shard_map/pallas_call | solution.py:1057
  604.6 0.0 copy-start.9
  604.6 1.5 copy.55
  606.2 0.1 copy.56
  606.3 0.2 copy.57
  606.5 0.1 convert_select_fusion
  606.6 1.8 copy.60
  608.4 0.6 slice_bitcast_fusion.1
  609.0 0.6 slice.23
  609.6 0.5 copy.53
  610.1 1.5 copy.54
  611.6 3.0 copy.59
  614.5 0.0 copy-done.4
  614.5 0.3 copy.51
  614.8 0.1 copy.52
  615.0 0.0 copy-start
  615.0 1.6 copy.58
  616.6 1.6 bitcast_convert_fusion
  618.2 0.0 copy-done.8
  618.2 0.8 bitcast_convert_fusion.1
  619.0 0.0 copy-done.7
  619.0 0.8 copy.64
  619.8 0.0 copy-done.6
  619.8 0.8 copy.65
  (15 shorter events, 0.0 us)
Async XLA Ops:
  2.0 3.4 copy-start.2
  6.1 1.4 copy-start.3
  7.5 1.7 copy-start.10
  7.5 1.7 copy-start.15
  7.5 1.9 copy-start.5
  7.9 3.3 copy-start.11
  7.9 3.3 copy-start.12
  7.9 3.3 copy-start.13
  7.9 3.9 copy-start.16
  7.9 4.1 copy-start.17
  604.6 1.6 copy-start.9
  606.6 1.8 copy-start.14
  606.6 3.0 copy-start.1
  611.6 3.0 copy-start.4
  615.0 1.6 copy-start
  616.6 1.6 copy-start.8
  616.6 2.4 copy-start.7
  616.6 3.2 copy-start.6

commit v3 on v2

--- a/solution.py
+++ b/solution.py
@@ -22,7 +22,7 @@
 NN, NT, TN = (((1,), (0,)), ((), ())), (((1,), (1,)), ((), ())), (((0,), (0,)), ((), ()))
 ATTN, CROSS, FFN = 0, 1, 2
 QKV, FIN, FOUT, CQKV, OUT, COUT = range(6)
-KIND_MATS = {ATTN: (QKV, OUT), CROSS: (CQKV, COUT), FFN: (FIN, FOUT)}
+KIND_MATS = {ATTN: (QKV, OUT), CROSS: (CQKV, COUT), FFN: (FOUT, FIN)}
 DECODER_MATS = (CQKV, COUT)
 
 
@@ -147,11 +147,13 @@
         rsb_r=dma((2, NH, K)),
         gr_s=dma((nst, 6)),
         gr_r=dma((nst, 6)),
-        credit=pltpu.SemaphoreType.REGULAR((nst, 3)),
+        credit=pltpu.SemaphoreType.REGULAR((nst, 6)),
         home_s=dma((6, tz)),
         home_r=dma((6, max(TPN, C))),
         sig_s=dma((L, NH)),
         sig_r=dma((TPN,)),
+        fin_s=dma((NH,)),
+        fin_r=dma((TPN,)),
         sm1_s=dma((TPN,)),
         sm1_rs=dma((TPN,)),
         sm2_s=dma((NU,)),
@@ -159,22 +161,23 @@
         out_l=dma((L,)),
         smo_l=dma((1,)),
     )
-    slots = 2 if nst == 2 else 1
+    lagged = nst == 2
+    slots = 2 if lagged else 1
     for m, block in mat_block.items():
         scratch["w%d" % m] = vm((LD if m in DECODER_MATS else L,) + two[m] + block, bf16)
         scratch["g%d" % m] = vm((slots,) + two[m] + block, bf16)
         scratch["st%d" % m] = vm((2 ** (len(two[m]) - nst),) + block, bf16)
         for j in range(1, nst + 1):
             scratch["r%d_%d" % (m, j)] = vm(two[m][j:] + block, bf16)
-    in_names = ["src", "x2", "cot", "auxi", "dirwi", "normsi", "aq", "ai", "af", "ac", "woi", "wcoi"]
-    out_names = ["out", "sig", "hq", "hi", "hf", "hc", "hwo", "hwco", "smout"]
+    in_names = ["src", "x2", "cot", "auxi", "dirwi", "normsi", "aq", "ai", "af", "ac", "woi"]
+    out_names = ["out", "sig", "hq", "hi", "hf", "hc", "hwo", "smout"]
     scratch_names = list(scratch)
 
     def kernel(*refs):
         n = types.SimpleNamespace(**dict(zip(in_names + out_names + scratch_names, refs)))
         W = {m: getattr(n, "w%d" % m) for m in mat_block}
         A = {QKV: n.aq, FIN: n.ai, FOUT: n.af, CQKV: n.ac}
-        H = {QKV: n.hq, FIN: n.hi, FOUT: n.hf, CQKV: n.hc, OUT: n.hwo, COUT: n.hwco}
+        H = {QKV: n.hq, FIN: n.hi, FOUT: n.hf, CQKV: n.hc, OUT: n.hwo, COUT: n.hc}
         G = {m: getattr(n, "g%d" % m) for m in mat_block}
         ST = {m: getattr(n, "st%d" % m) for m in mat_block}
         RB = {m: [None] + [getattr(n, "r%d_%d" % (m, j)) for j in range(1, nst + 1)] for m in mat_block}
@@ -249,21 +252,28 @@
                 wait(e, n.init_s.at[i])
                 wait(e, n.init_r.at[i])
 
-        first_start(2)
-        first_start(0)
-
         def wreg(m, l, fixed):
             idx = tuple(fixed.get(b, slice(None)) for b in mat_bits[m])
             return W[m].at[(l - half if m in DECODER_MATS else l,) + idx]
 
         mine = {b: bit[b] for b in range(NB)}
 
+        def parts_of(m, rank):
+            if m in (FIN, FOUT):
+                return [((rank,), (slice(None), slice(None)))]
+            return [
+                ((slice(None), pl.ds(mul(part * TPN + rank, CW), CW)), (slice(None), slice(part * CW, part * CW + CW)))
+                for part in range(3)
+            ]
+
         def a2a_start(m):
             dst = wreg(m, s, mine)
-            local(A[m].at[r], dst, n.a2a_r.at[m, s, zl]).start()
+            for here, there in parts_of(m, r):
+                local(A[m].at[here], dst.at[there], n.a2a_r.at[m, s, zl]).start()
             for j in range(1, TPN):
                 to = rm(r + j, TPN)
-                remote(A[m].at[to], dst, n.a2a_s.at[m, j], n.a2a_r.at[m, s, zl], place(to, g)).start()
+                for here, there in parts_of(m, to):
+                    remote(A[m].at[here], dst.at[there], n.a2a_s.at[m, j], n.a2a_r.at[m, s, zl], place(to, g)).start()
 
         def group_bits(m, group):
             count = len(mat_bits[m])
@@ -271,9 +281,10 @@
 
         def out_pieces(m):
             rank = dv(d, q)
+            first = 3 * D if m == COUT else 0
             for c in range(C):
                 group = rm(d, q) * C + c
-                yield c, pl.ds(c * cw, cw), group, rank, (rank == r) & (group == g)
+                yield c, pl.ds(first + c * cw, cw), group, rank, (rank == r) & (group == g)
 
         def out_start(m, src):
             for c, span, group, rank, here in out_pieces(m):
@@ -337,7 +348,7 @@
                         if m == OUT:
                             out_start(OUT, n.woi)
                         elif m == COUT:
-                            out_start(COUT, n.wcoi)
+                            out_start(COUT, n.ac)
                         else:
                             a2a_start(m)
 
@@ -359,7 +370,11 @@
 
             groups(t, last)
 
-        @pl.loop(0, ahead[0])
+        feed(-ahead[0])
+        first_start(2)
+        first_start(0)
+
+        @pl.loop(1, ahead[0])
         def _(i):
             feed(i - ahead[0])
 
@@ -522,6 +537,22 @@
             th = jnp.tanh(c0 * (v + c1 * (v * v * v)))
             return 0.5 * (1.0 + th) + 0.5 * v * (1.0 - th * th) * (c0 * (1.0 + 3.0 * c1 * v * v))
 
+        def rows_home(src, dst, send, recv, l, h, act):
+            here = (l == s) & (h == zl)
+
+            @pl.when(here)
+            def _():
+                if act == "start":
+                    local(src, dst.at[own], recv.at[r]).start()
+
+            @pl.when(jnp.logical_not(here))
+            def _():
+                if act == "start":
+                    to = (l, with_bit(PAIR_BIT, h) if tz == 2 else d)
+                    remote(src, dst.at[own], send, recv.at[r], to).start()
+                else:
+                    wait(src, send)
+
         def self_forward(l, t, xi, causal, alpha, into):
             feed(t)
             ready(t)
@@ -580,18 +611,28 @@
                 value = alpha * n.res[h] + rs_finish(0, h)
                 result = ln_forward(t, h, value, norm_row(l, 1), norm_row(l, 3))
                 n.xbuf[xo, h, own] = result.astype(bf16)
-                tp_start(n.xbuf.at[xo, h], h, 1)
+
+                @pl.when(l < L - 1)
+                def _():
+                    tp_start(n.xbuf.at[xo, h], h, 1)
+
+                @pl.when(l == L - 1)
+                def _():
+                    rows_home(n.xbuf.at[xo, h, own], n.out, n.fin_s.at[h], n.fin_r, L - 1, h, "start")
 
             def third(h):
                 tp_finish(n.xbuf.at[xo, h], h, 1)
 
             halves(first)
             halves(second)
-            halves(third)
-
-            @pl.when(s == l)
+
+            @pl.when(l < L - 1)
             def _():
-                local(n.xbuf.at[xo, zl], n.out, n.out_l.at[0]).start()
+                halves(third)
+
+                @pl.when(s == l)
+                def _():
+                    local(n.xbuf.at[xo, zl], n.out, n.out_l.at[0]).start()
 
         for i in (2, 0):
             first_wait(i)
@@ -626,38 +667,44 @@
             b = back_steps[j - 1]
             return (s, with_bit(b, 1 - bit[b]))
 
-        def gr_start(j, kd, mats, l):
+        def gr_start(j, m, l):
             @pl.when(l != L - 1)
             def _():
-                pl.semaphore_wait(n.credit.at[j - 1, kd], 1)
-
-            for m in mats:
-                fixed = {b: bit[b] for b in back_steps[: j - 1]}
-                fixed[back_steps[j - 1]] = 1 - bit[back_steps[j - 1]]
-                remote(
-                    gregion(m, l, fixed), RB[m][j], n.gr_s.at[j - 1, m], n.gr_r.at[j - 1, m], partner(j)
-                ).start()
+                pl.semaphore_wait(n.credit.at[j - 1, m], 1)
+
+            fixed = {b: bit[b] for b in back_steps[: j - 1]}
+            fixed[back_steps[j - 1]] = 1 - bit[back_steps[j - 1]]
+            remote(gregion(m, l, fixed), RB[m][j], n.gr_s.at[j - 1, m], n.gr_r.at[j - 1, m], partner(j)).start()
 
         def blocks_of(count):
             return [
                 tuple((i >> b) & 1 for b in reversed(range(count))) for i in range(1 << count)
             ]
 
-        def gr_finish(j, kd, mats, l):
-            for m in mats:
-                wait(RB[m][j], n.gr_r.at[j - 1, m])
-                mine_part = gregion(m, l, {b: bit[b] for b in back_steps[:j]})
-                for idx in blocks_of(len(mat_bits[m]) - j):
-                    value = mine_part[idx].astype(f32) + RB[m][j][idx].astype(f32)
-                    if j == nst:
-                        ST[m][idx if idx else 0] = value.astype(bf16)
-                    else:
-                        mine_part[idx] = value.astype(bf16)
-                wait(RB[m][j], n.gr_s.at[j - 1, m])
-
-            @pl.when(l != (half if kd == CROSS else 0))
+        def gr_finish(j, m, l):
+            wait(RB[m][j], n.gr_r.at[j - 1, m])
+            mine_part = gregion(m, l, {b: bit[b] for b in back_steps[:j]})
+            for idx in blocks_of(len(mat_bits[m]) - j):
+                value = mine_part[idx].astype(f32) + RB[m][j][idx].astype(f32)
+                if j == nst:
+                    ST[m][idx if idx else 0] = value.astype(bf16)
+                else:
+                    mine_part[idx] = value.astype(bf16)
+            wait(RB[m][j], n.gr_s.at[j - 1, m])
+
+            @pl.when(l != (half if m in DECODER_MATS else 0))
             def _():
-                pl.semaphore_signal(n.credit.at[j - 1, kd], inc=1, device_id=partner(j), device_id_type=MESH)
+                pl.semaphore_signal(n.credit.at[j - 1, m], inc=1, device_id=partner(j), device_id_type=MESH)
+
+            if j < nst:
+                gr_start(j + 1, m, l)
+            else:
+                for z in range(ST[m].shape[0]):
+                    home(m, l, z, "start")
+
+        def homes_wait(m, l):
+            for z in range(ST[m].shape[0]):
+                home(m, l, z, "wait")
 
         def home(m, l, z, act):
             src = ST[m].at[z]
@@ -665,45 +712,55 @@
                 piece = rm(g, C)
                 to = (l, r * q + dv(g, C))
                 here = (l == s) & (to[1] == d)
-                dst, slot = H[m].at[:, pl.ds(mul(piece, cw), cw)], piece
+                first = 3 * D if m == COUT else 0
+                copies = [(src, H[m].at[:, pl.ds(pl.multiple_of(first + piece * cw, cw), cw)])]
+                slot = piece
             else:
                 to = (l, with_bit(PAIR_BIT, z) if tz == 2 else d)
                 here = (l == s) & (zl == z) if tz == 2 else l == s
-                dst, slot = H[m].at[r], r
-
+                copies = [(src.at[b], H[m].at[a]) for a, b in parts_of(m, r)]
+                slot = r
             if act == "wait":
                 wait(src, n.home_s.at[m, z])
                 return
 
             @pl.when(here)
             def _():
-                local(src, dst, n.home_s.at[m, z]).start()
+                for a, b in copies:
+                    local(a, b, n.home_s.at[m, z]).start()
 
             @pl.when(jnp.logical_not(here))
             def _():
-                remote(src, dst, n.home_s.at[m, z], n.home_r.at[m, slot], to).start()
-
-        behind = BEHIND if nst == 2 else tuple(range(1, nst + 1))
+                for a, b in copies:
+                    remote(a, b, n.home_s.at[m, z], n.home_r.at[m, slot], to).start()
+
+        def homes_wait(m, l):
+            for z in range(ST[m].shape[0]):
+                home(m, l, z, "wait")
 
         def process(u):
+            if not lagged:
+                return
+
             def old(kd, mats, l):
                 for m in mats:
-                    for z in range(ST[m].shape[0]):
-                        home(m, l, z, "wait")
-
-            groups(T - 1 - (u - behind[nst - 1] - 1), old)
-            for j in range(nst, 0, -1):
+                    homes_wait(m, l)
+
+            groups(T - 1 - (u - BEHIND[nst - 1] - 1), old)
+            for j in range(1, nst + 1):
 
                 def fn(kd, mats, l, j=j):
-                    gr_finish(j, kd, mats, l)
-                    if j < nst:
-                        gr_start(j + 1, kd, mats, l)
-                    else:
-                        for m in mats:
-                            for z in range(ST[m].shape[0]):
-                                home(m, l, z, "start")
-
-                groups(T - 1 - (u - behind[j - 1]), fn)
+                    for m in mats:
+                        gr_finish(j, m, l)
+
+                groups(T - 1 - (u - BEHIND[j - 1]), fn)
+
+        def send_grad(m, l):
+            gr_start(1, m, l)
+            if not lagged:
+                for j in range(1, nst + 1):
+                    gr_finish(j, m, l)
+                homes_wait(m, l)
 
         def weight_grad(m, l, lefts, rights):
             rows, cols = mat_block[m]
@@ -764,10 +821,11 @@
                 n.actb[h] = gelu(before).astype(bf16)
 
             halves(first)
+            weight_grad(FOUT, l, [each(n.actb)], [each(gag)])
             process(u)
-            weight_grad(FOUT, l, [each(n.actb)], [each(gag)])
+            send_grad(FOUT, l)
             weight_grad(FIN, l, [each(n.hb.at[l])], [each(n.gpre)])
-            gr_start(1, FFN, KIND_MATS[FFN], l)
+            send_grad(FIN, l)
 
             def second(h):
                 n.gy[h] = alpha * n.res[h] + rs_finish(0, h)
@@ -792,8 +850,9 @@
                 n.gmem[h] += dot(n.gqkv[h, :, CW:], weight(CQKV, l, CW), NT)
 
             halves(first)
+            out_grad(COUT, l, each(n.cosv.at[ld]), each(gag))
             process(u)
-            out_grad(COUT, l, each(n.cosv.at[ld]), each(gag))
+            send_grad(COUT, l)
             weight_grad(
                 CQKV,
                 l,
@@ -803,7 +862,7 @@
                     [n.gqkv.at[h, :, pl.ds(CW, 2 * CW)] for h in range(NH)],
                 ],
             )
-            gr_start(1, CROSS, KIND_MATS[CROSS], l)
+            send_grad(CQKV, l)
 
             def second(h):
                 n.gy[h] = DECODER_ALPHA * n.res[h] + rs_finish(0, h)
@@ -811,21 +870,7 @@
             halves(second)
 
         def sig_copy(l, h, act):
-            here = (l == s) & (h == zl)
-            src = n.gxo.at[l, h]
-
-            @pl.when(here)
-            def _():
-                if act == "start":
-                    local(src, n.sig.at[own], n.sig_r.at[r]).start()
-
-            @pl.when(jnp.logical_not(here))
-            def _():
-                if act == "start":
-                    to = (l, with_bit(PAIR_BIT, h) if tz == 2 else d)
-                    remote(src, n.sig.at[own], n.sig_s.at[l, h], n.sig_r.at[r], to).start()
-                else:
-                    wait(src, n.sig_s.at[l, h])
+            rows_home(n.gxo.at[l, h], n.sig, n.sig_s.at[l, h], n.sig_r, l, h, act)
 
         def self_backward(l, t, u, xi, causal, alpha):
             gag = branch_grad(t, l, u, 0, 2)
@@ -841,10 +886,11 @@
                 rs_start(0, h, lambda row: dot(n.gqkv[h, pl.ds(row, HB)], weight(QKV, l), NT))
 
             halves(first)
+            out_grad(OUT, l, each(n.osv.at[l]), each(gag))
             process(u)
-            out_grad(OUT, l, each(n.osv.at[l]), each(gag))
+            send_grad(OUT, l)
             weight_grad(QKV, l, [each(n.xbuf.at[xi])], [each(n.gqkv)])
-            gr_start(1, ATTN, KIND_MATS[ATTN], l)
+            send_grad(QKV, l)
 
             def second(h):
                 grad = (alpha * n.res[h] + rs_finish(0, h)).astype(bf16)
@@ -891,6 +937,8 @@
             u = 3 * LD + 2 * i
             ffn_backward(l, 2 * l + 1, u, ENCODER_ALPHA)
             self_backward(l, 2 * l, u + 1, l, False, ENCODER_ALPHA)
+
+        process(T)
 
         for rank in range(TPN):
             for g2 in range(NU):
@@ -902,9 +950,11 @@
             to = rm(r + j, TPN)
             remote(n.sm1.at[to], n.sm1r.at[j], n.sm1_s.at[j], n.sm1_rs.at[j], place(to, g)).start()
 
-        @pl.loop(0, behind[nst - 1] + 1)
-        def _(i):
-            process(T + i)
+        if lagged:
+
+            @pl.loop(1, BEHIND[nst - 1] + 1)
+            def _(i):
+                process(T + i)
 
         total_small = n.sm1[r]
         for j in range(1, TPN):
@@ -927,7 +977,7 @@
         def home_wait(m):
             for j in range(1, TPN):
                 rank = rm(r + j, TPN)
-                wait(H[m].at[rank], n.home_r.at[m, rank])
+                wait(ST[m].at[0], n.home_r.at[m, rank])
 
         def home_wait_out(m):
             for c, span, group, rank, here in out_pieces(m):
@@ -947,7 +997,17 @@
 
         for rank in range(TPN):
             wait(n.sig.at[pl.ds(rank * RR, RR)], n.sig_r.at[rank])
-        wait(n.out, n.out_l.at[0])
+        @pl.when(s < L - 1)
+        def _():
+            wait(n.out, n.out_l.at[0])
+
+        @pl.when(s == L - 1)
+        def _():
+            for rank in range(TPN):
+                wait(n.out.at[pl.ds(rank * RR, RR)], n.fin_r.at[rank])
+
+        for h in range(NH):
+            rows_home(n.xbuf.at[L + 1, h, own], n.out, n.fin_s.at[h], n.fin_r, L - 1, h, "wait")
         for l in range(L):
             for h in range(NH):
                 sig_copy(l, h, "wait")
@@ -959,12 +1019,12 @@
             wait(n.norms.at[0], n.norm_s.at[j])
         for j in range(1, TPN):
             for m in (QKV, FIN, FOUT):
-                wait(A[m].at[0], n.a2a_s.at[m, j])
+                wait(ST[m].at[0], n.a2a_s.at[m, j])
 
         @pl.when(s >= half)
         def _():
             for j in range(1, TPN):
-                wait(A[CQKV].at[0], n.a2a_s.at[CQKV, j])
+                wait(ST[CQKV].at[0], n.a2a_s.at[CQKV, j])
 
         for m in (OUT, COUT):
             for c, span, group, rank, here in out_pieces(m):
@@ -972,7 +1032,7 @@
 
                 @pl.when(sends)
                 def _():
-                    wait(n.woi.at[:, span], n.wo_s.at[m - OUT, c])
+                    wait(ST[m].at[0], n.wo_s.at[m - OUT, c])
 
         @pl.loop(0, L)
         def _(l):
@@ -995,11 +1055,10 @@
     outs = [
         sd(R, D),
         sd(R, D),
-        blocks(QKV, TPN),
+        sd(p.rb, 3 * D),
         blocks(FIN, TPN),
         blocks(FOUT, TPN),
-        blocks(CQKV, TPN),
-        sd(p.rb, D),
+        sd(p.rb, 4 * D),
         sd(p.rb, D),
         sd(16, 128, dtype=f32),
     ]
@@ -1049,41 +1108,32 @@
         norms = jnp.concatenate(
             (norm_gain[0], norm_bias[0], cross_norm[0], jnp.zeros((2, width), bf16)), axis=0
         ).astype(f32)
-        aq = attn_in[0].reshape(p.rb, 3, p.TPN, p.CW).transpose(2, 0, 1, 3).reshape(p.TPN, p.rb, 3 * p.CW)
-        cross = cross_weight[0][:, : 3 * width]
-        ac = cross.reshape(p.rb, 3, p.TPN, p.CW).transpose(2, 0, 1, 3).reshape(p.TPN, p.rb, 3 * p.CW)
         ai = ffn_in[0].reshape(p.rb, p.ND, p.TPN, p.fb).transpose(2, 0, 1, 3).reshape(p.TPN, p.rb, p.FB)
         af = ffn_out[0].reshape(p.TPN, p.fb, width)
-        out, sig, hq, hi, hf, hc, hwo, hwco, small = build(p)(
+        out, sig, hq, hi, hf, hc, hwo, small = build(p)(
             source.reshape(p.R, width),
             x2,
             cotangent.reshape(p.R, width),
             aux,
             dirw,
             norms,
-            aq,
+            attn_in[0],
             ai,
             af,
-            ac,
+            cross_weight[0],
             attn_out[0],
-            cross_weight[0][:, 3 * width :],
         )
         decoder = section >= p.half
-
-        def heads_back(value):
-            value = value.reshape(p.TPN, p.rb, 3, p.CW).transpose(1, 2, 0, 3)
-            return value.reshape(1, p.rb, 3 * width).astype(f32)
 
         g_in = hi.reshape(p.TPN, p.rb, p.ND, p.fb).transpose(1, 2, 0, 3).reshape(1, p.rb, p.FF).astype(f32)
         g_out = hf.reshape(1, p.TPN * p.fb, width).astype(f32)
         g_wo = hwo.astype(f32)[None]
-        g_cross = jnp.concatenate((heads_back(hc), hwco.astype(f32)[None]), axis=2)
-        g_cross = jnp.where(decoder, g_cross, jnp.zeros_like(g_cross))
+        g_cross = jnp.where(decoder, hc.astype(f32), jnp.zeros(hc.shape, f32))[None]
         small = small[:, : p.cols]
         return (
             out.reshape(1, pairs, seq, width),
             sig.reshape(1, pairs, seq, width),
-            heads_back(hq),
+            hq.astype(f32)[None],
             g_wo,
             g_in,
             g_out,

time: 621 us -> 615 us (level)
  local copies, waits for them, and re-layouts: 22.8 us -> 14.2 us
where the time goes in v3:
time: 615 us; the launch traced here: 614 us
  Pallas kernels  591 us (96%)
  local copies, waits for them, and re-layouts  14.2 us (2%)
  other arithmetic  7.75 us (1%)
    pallas_call x1, Pallas kernels, body(): build(p)  591 us

profile of v3, /device:TPU:0, one launch (start us, length us, event | category | flops | bytes accessed | tf_op | source)
XLA Modules:
  0.0 614.3 jit_solution(10816102490560915340)
XLA Ops:
  0.6 1.6 copy.28
  2.3 0.0 copy-start.7
  2.3 0.0 copy-start.11
  2.3 0.0 copy-start.3
  2.3 0.1 copy.29
  2.4 0.0 copy-start.8
  2.4 0.0 copy-start.9
  2.4 0.0 copy-start.10
  2.4 0.0 copy-start.12
  2.4 0.0 copy-start.13
  2.5 1.3 copy.30.refs_7_
  3.8 0.0 copy-done.7
  3.8 0.0 copy-done.11
  3.8 0.2 fusion.1
  4.0 0.0 copy-done.3
  4.0 0.9 add_convert_fusion
  4.9 0.1 fusion
  5.0 0.7 broadcast_in_dim.47.refs_4_
  5.7 0.1 pad.3.clone
  5.8 0.0 copy-done.8
  5.8 0.0 copy-done.9
  5.8 0.0 copy-done.10
  5.8 0.7 maximum_convert_fusion.refs_5_
  6.5 0.0 copy-done.12
  6.5 0.1 fusion.2
  6.5 0.1 reshape.159
  6.6 0.0 copy-done.13
  6.6 0.1 fusion.3
  6.7 0.1 reshape.160
  6.8 0.1 pad.6.clone
  6.9 0.7 maximum_maximum_fusion.refs_3_
  7.5 591.4 %shard_map.230 = (bf16[256,1024]{1,0:T(8,128)(2,1)}, bf16[256,1024]{1,0:T(8,128)(2,1)}, bf16[128,3072]{1,0:T(8,128)(2,1)}, bf16[8,128,512]{2,1,0:T(8,128)(2,1)},...) custom-call(bf16[256,1024]{1,0:T(8,128)(2,1)} %bitcast.48, ...), custom_call_target="tpu_custom_call" | custom-call | tf_op jit(solution)/shard_map/pallas_call | solution.py:1113
  598.9 1.4 slice_bitcast_fusion
  600.3 1.3 slice.15
  601.6 1.5 copy.31
  603.0 1.5 copy.32
  604.5 0.0 copy-start.1
  604.5 3.0 copy.33
  607.5 0.0 copy-start
  607.5 0.0 copy-done.1
  607.5 1.5 select_bitcast_fusion
  609.0 0.0 copy-start.2
  609.0 0.0 copy-done
  609.0 0.0 copy-start.6
  609.0 1.6 bitcast_convert_fusion
  610.6 0.0 copy-start.5
  610.6 0.0 copy-done.2
  610.6 0.0 copy-start.4
  610.6 1.3 bitcast_convert_fusion.1
  611.9 0.0 copy-done.6
  611.9 0.8 bitcast_convert_fusion.2
  612.7 0.0 copy-done.5
  612.7 0.8 copy.36
  613.5 0.0 copy-done.4
  613.5 0.8 copy.37
  (2 shorter events, 0.0 us)
Async XLA Ops:
  2.3 1.5 copy-start.7
  2.3 1.5 copy-start.11
  2.3 1.7 copy-start.3
  2.4 3.4 copy-start.8
  2.4 3.4 copy-start.9
  2.4 3.3 copy-start.10
  2.4 4.0 copy-start.12
  2.4 4.2 copy-start.13
  604.5 3.0 copy-start.1
  607.5 1.6 copy-start
  609.0 1.6 copy-start.2
  609.0 2.9 copy-start.6
  610.6 2.2 copy-start.5
  610.6 2.9 copy-start.4

commit v4 on v3

--- a/solution.py
+++ b/solution.py
@@ -10,7 +10,7 @@
 
 HEADS = 16
 GROUP = 8
-AHEAD = (4, 3, 2)
+AHEAD = (5, 4, 2)
 BEHIND = (2, 3)
 PAIR_BIT = 0
 ENCODER_ALPHA = 3.42
@@ -105,7 +105,6 @@
         osv=vm((L, NH, R, CW), bf16),
         cosv=vm((LD, NH, R, CW), bf16),
         pre=vm((L, NH, R, FB), bf16),
-        act=vm((R, FB), bf16),
         zs=vm((T, NH, RR, D), bf16),
         rstd=vm((T, NH, RR, 128), f32),
         res=vm((NH, RR, D), f32),
@@ -356,19 +355,15 @@
             for j in range(1, nst + 1):
 
                 def fn(kd, mats, l, j=j):
-                    for m in mats:
+                    for m in reversed(mats):
                         ag_wait(j - 1, m, l)
-                    for m in mats:
                         ag_start(j - 1, m, l)
 
                 groups(t + ahead[j], fn)
 
-        def ready(t):
-            def last(kd, mats, l):
-                for m in mats:
-                    ag_wait(nst, m, l)
-
-            groups(t, last)
+        def ready(l, *mats):
+            for m in mats:
+                ag_wait(nst, m, l)
 
         feed(-ahead[0])
         first_start(2)
@@ -555,7 +550,7 @@
 
         def self_forward(l, t, xi, causal, alpha, into):
             feed(t)
-            ready(t)
+            ready(l, QKV, OUT)
 
             def first(h):
                 n.qkv[l, h] = dot(n.xbuf[xi, h], weight(QKV, l), NN).astype(bf16)
@@ -575,7 +570,7 @@
 
         def cross_forward(l, t):
             feed(t)
-            ready(t)
+            ready(l, CQKV, COUT)
             ld = l - half
 
             def first(h):
@@ -598,14 +593,16 @@
 
         def ffn_forward(l, t, xo, alpha):
             feed(t)
-            ready(t)
+            ready(l, FIN)
 
             def first(h):
                 tp_finish(n.hb.at[l, h], h)
                 before = dot(n.hb[l, h], weight(FIN, l), NN)
                 n.pre[l, h] = before.astype(bf16)
-                n.act[...] = gelu(before).astype(bf16)
-                rs_start(0, h, lambda row: dot(n.act[pl.ds(row, HB)], weight(FOUT, l), NN))
+                n.actb[h] = gelu(before).astype(bf16)
+
+            def send(h):
+                rs_start(0, h, lambda row: dot(n.actb[h, pl.ds(row, HB)], weight(FOUT, l), NN))
 
             def second(h):
                 value = alpha * n.res[h] + rs_finish(0, h)
@@ -624,6 +621,8 @@
                 tp_finish(n.xbuf.at[xo, h], h, 1)
 
             halves(first)
+            ready(l, FOUT)
+            halves(send)
             halves(second)
 
             @pl.when(l < L - 1)

time: 615 us -> 615 us (level)
  no operation moved by 1% of the time
where the time goes in v4:
time: 615 us
  Pallas kernels  592 us (96%)
  local copies, waits for them, and re-layouts  14.2 us (2%)
  other arithmetic  7.75 us (1%)
    pallas_call x1, Pallas kernels, body(): build(p)  592 us

profile of v4, /device:TPU:0, one launch (start us, length us, event | category | flops | bytes accessed | tf_op | source)
XLA Modules:
  0.0 615.2 jit_solution(10834003262064865910)
XLA Ops:
  0.6 1.6 copy.28
  2.3 0.0 copy-start.7
  2.3 0.0 copy-start.11
  2.3 0.0 copy-start.3
  2.3 0.1 copy.29
  2.4 0.0 copy-start.8
  2.4 0.0 copy-start.9
  2.4 0.0 copy-start.10
  2.4 0.0 copy-start.12
  2.4 0.0 copy-start.13
  2.5 1.3 copy.30.refs_7_
  3.8 0.0 copy-done.7
  3.8 0.0 copy-done.11
  3.8 0.2 fusion.1
  4.0 0.0 copy-done.3
  4.0 0.9 add_convert_fusion
  4.9 0.1 fusion
  5.0 0.7 broadcast_in_dim.47.refs_4_
  5.7 0.1 pad.3.clone
  5.8 0.0 copy-done.8
  5.8 0.0 copy-done.9
  5.8 0.0 copy-done.10
  5.8 0.7 maximum_convert_fusion.refs_5_
  6.5 0.0 copy-done.12
  6.5 0.1 fusion.2
  6.5 0.1 reshape.159
  6.6 0.0 copy-done.13
  6.6 0.1 fusion.3
  6.7 0.1 reshape.160
  6.8 0.1 pad.6.clone
  6.9 0.7 maximum_maximum_fusion.refs_3_
  7.5 592.3 %shard_map.230 = (bf16[256,1024]{1,0:T(8,128)(2,1)}, bf16[256,1024]{1,0:T(8,128)(2,1)}, bf16[128,3072]{1,0:T(8,128)(2,1)}, bf16[8,128,512]{2,1,0:T(8,128)(2,1)},...) custom-call(bf16[256,1024]{1,0:T(8,128)(2,1)} %bitcast.48, ...), custom_call_target="tpu_custom_call" | custom-call | tf_op jit(solution)/shard_map/pallas_call | solution.py:1112
  599.8 1.4 slice_bitcast_fusion
  601.2 1.3 slice.15
  602.4 1.5 copy.31
  603.9 1.5 copy.32
  605.4 0.0 copy-start.1
  605.4 3.0 copy.33
  608.4 0.0 copy-start
  608.4 0.0 copy-done.1
  608.4 1.5 select_bitcast_fusion
  609.9 0.0 copy-start.2
  609.9 0.0 copy-done
  609.9 0.0 copy-start.6
  609.9 1.6 bitcast_convert_fusion
  611.5 0.0 copy-start.5
  611.5 0.0 copy-done.2
  611.5 0.0 copy-start.4
  611.5 1.3 bitcast_convert_fusion.1
  612.8 0.0 copy-done.6
  612.8 0.8 bitcast_convert_fusion.2
  613.6 0.0 copy-done.5
  613.6 0.8 copy.36
  614.4 0.0 copy-done.4
  614.4 0.8 copy.37
  (2 shorter events, 0.0 us)
Async XLA Ops:
  2.3 1.5 copy-start.7
  2.3 1.5 copy-start.11
  2.3 1.7 copy-start.3
  2.4 3.4 copy-start.8
  2.4 3.4 copy-start.9
  2.4 3.3 copy-start.10
  2.4 4.0 copy-start.12
  2.4 4.2 copy-start.13
  605.4 3.0 copy-start.1
  608.4 1.6 copy-start
  609.9 1.6 copy-start.2
  609.9 2.9 copy-start.6
  611.5 2.2 copy-start.5
  611.5 2.9 copy-start.4
